TPU v7x, 128 devices: a whole 4x4x4 slice. The times are simulated.
128 devices in a mesh: row: 8 (over x, z_lo), col: 4 (over z_hi, core), depth: 4 (over y).
Axes of the slice: x: 4, y: 4, z: 4 (z_hi: 2, z_lo: 2; z = z_hi * 2 + z_lo), core: 2. Of those that a mesh axis runs over, the one named last changes fastest.
Arguments:
- out_grad: bfloat16 [131072, 512], P(('row', 'col'), 'depth'), may hold values from -6 to 6
- relu_mask: int32 [131072, 512], P(('row', 'col'), 'depth'), may hold values 0 or 1
- aggregated: bfloat16 [131072, 512], P(('row', 'col'), 'depth'), may hold values from -0.015625 to 0.015625
- weight: bfloat16 [512, 512], P(None, 'depth'), may hold values from -0.25 to 0.25
- tile_values: bfloat16 [8, 4, 544, 128, 128], P('row', 'col'), may hold values from -0.1875 to 0.1875
- tile_rows: int32 [8, 4, 544], P('row', 'col'), may hold values from 0 to 127, as said below
- tile_cols: int32 [8, 4, 544], P('row', 'col'), may hold values from 0 to 1023, as said below
- tile_count: int32 [8, 4], P('row', 'col'), may hold values from 0 to 544, as said below
Outputs:
- grad_input: bfloat16 [131072, 512], P(('row', 'col'), 'depth')
- grad_weight: float32 [512, 512], P(None, 'depth')
Inputs may be any that keep to these rules, and one draw needn't show every extreme that they name: Slots below a device's count hold distinct tiles of the band: tile_cols is (r * 128 + tile_rows + k) mod 1024 for some k from -8 to 8, and tile_cols % 4 equals the device's col index c; slots at or after the count hold other coordinates of the same ranges and are to be ignored. `tile_cols`: see tile_rows. `tile_count`: some device is full in every draw.
All inputs are finite; a program needn't handle non-finite values. No bound on the sum of `relu_mask` on one device may be relied on, other than what follows from the above.
Results may differ from a plain program's by a relative error of at most 0.0049.
Values may be sent and summed in bfloat16 or wider, within the bound.
No kernel may reach another device: no remote copies, remote signals or barrier semaphores. Data moves between devices by JAX's collectives and lax.ppermute only.
A program may use at most 192 MiB of HBM per device.

v0:
```python
import jax
import jax.numpy as jnp
from jax import lax
from jax.sharding import PartitionSpec as P

BW = 8
RB = 128


def with_halo(cells, sides, width):
    for axis, dim in sides:
        count = lax.axis_size(axis)
        head = lax.slice_in_dim(cells, 0, width, axis=dim)
        tail = lax.slice_in_dim(cells, cells.shape[dim] - width, cells.shape[dim], axis=dim)
        cells = jnp.concatenate(
            [
                lax.ppermute(tail, axis, [(i, (i + 1) % count) for i in range(count)]),
                cells,
                lax.ppermute(head, axis, [((i + 1) % count, i) for i in range(count)]),
            ],
            axis=dim,
        )
    return cells


def local(out_grad, relu_mask, aggregated, weight, tile_values, tile_rows, tile_cols, tile_count):
    out_masked = out_grad * relu_mask.astype(jnp.bfloat16)
    owned_rows = out_masked.shape[0]
    feat_width = out_masked.shape[1]
    tile_size = tile_values.shape[-1]
    col_blocks = owned_rows // tile_size
    col_count = lax.axis_size("col")
    row_count = lax.axis_size("row")
    stripe_id = lax.axis_index("row")
    stripe_grad = lax.all_gather(out_masked, "col", axis=0, tiled=True)
    stripe_grad = stripe_grad.reshape(col_count * col_blocks, tile_size, feat_width)
    row_index = tile_rows[0, 0]
    col_index = tile_cols[0, 0]
    live_count = tile_count[0, 0]
    slot_count = row_index.shape[0]
    slot_live = jnp.arange(slot_count, dtype=jnp.int32) < live_count
    source = row_index % col_count * col_blocks + row_index // col_count
    picked = jnp.take(stripe_grad, source, axis=0)
    picked = jnp.where(slot_live[:, None, None], picked, jnp.zeros_like(picked))
    contrib = jnp.einsum(
        "sij,sif->sjf", tile_values[0, 0], picked, preferred_element_type=jnp.float32
    )
    placed = col_index % RB // col_count
    blocks_all = RB * row_count
    global_rows = stripe_id * RB + row_index
    offset = (col_index - global_rows + BW) % blocks_all - BW
    target = global_rows + offset
    direction = jnp.where(
        target >= (stripe_id + 1) * RB, 2, jnp.where(target < stripe_id * RB, 0, 1)
    )
    segment = direction * col_blocks + placed
    buffer = jax.ops.segment_sum(contrib, segment, num_segments=3 * col_blocks)
    padded = with_halo(buffer.reshape(3, owned_rows, feat_width), (("row", 0),), 1)
    summed = padded[0] + padded[2] + padded[4]
    spread = summed.astype(jnp.bfloat16)
    partial_terms = lax.dot_general(
        spread, weight, (((1,), (1,)), ((), ())), preferred_element_type=jnp.float32
    )
    grad_input = lax.psum_scatter(partial_terms, "depth", scatter_dimension=1, tiled=True).astype(
        jnp.bfloat16
    )
    weight_terms = lax.dot_general(
        lax.all_gather(aggregated, "depth", axis=1, tiled=True),
        out_masked,
        (((0,), (0,)), ((), ())),
        preferred_element_type=jnp.float32,
    )
    grad_weight = lax.psum(weight_terms, ("row", "col"))
    return (grad_input, grad_weight)


def solution(mesh):
    placed = (
        P(("row", "col"), "depth"),
        P(("row", "col"), "depth"),
        P(("row", "col"), "depth"),
        P(None, "depth"),
        P("row", "col", None, None, None),
        P("row", "col", None),
        P("row", "col", None),
        P("row", "col"),
    )
    return jax.shard_map(
        local,
        mesh=mesh,
        in_specs=placed,
        out_specs=(P(("row", "col"), "depth"), P(None, "depth")),
        check_vma=False,
    )
```

profile of v0, /device:TPU:0, one launch (start us, length us, event | category | flops | bytes accessed | tf_op | source)
XLA Modules:
  0.0 479.9 jit_solution(3465039100072656039)
XLA Ops:
  7.2 0.0 all-gather.3.cloned.1.call-start
  7.2 3.0 convert_multiply_fusion
  10.3 0.0 all-gather.5.cloned.1.call-start
  10.3 0.7 all-gather.5.cloned.1.call-update
  11.8 0.1 fusion.20
  11.9 39.7 %all-gather.3.cloned.1.call-done = bf16[16384,128]{1,0:T(8,128)(2,1)} async-done(((bf16[4096,128]{1,0:T(8,128)(2,1)}), bf16[16384,128]{1,0:T(8,128)(2,1)}) %all-gather.3.cloned.1.call-update) | async-done | bytes 4194320 | tf_op jit(solution)/shard_map/all_gather | solution.py:35
  51.6 17.8 %gather_fusion = bf16[544,128,128]{2,1,0:T(8,128)(2,1)} fusion(bf16[128,128,128]{2,1,0:T(8,128)(2,1)} %bitcast.59, s32[1024]{0:T(1024)S(1)} %pad_clamp_fusion), kind=kCustom, calls=%fused_computation | custom fusion | bytes 35653760 | tf_op jit(solution)/shard_map/jit(_take)/gather | solution.py:43
  69.4 27.0 %fusion.6 = f32[544,128,128]{1,2,0:T(8,128)} fusion(bf16[1,1,544,128,128]{4,3,2,1,0:T(8,128)(2,1)} %param.12, bf16[544,128,128]{2,1,0:T(8,128)(2,1)} %gather_fusion, pred[544]{0:T(1024)(128)(4,1)S(1)} %get-tuple-element.12, pred[544]{0:T(1024)(128)(4,1)S(1)} %get-tuple-element.11), kind=kOutput, calls=%fused_computation.8 | convolution fusion | flops 2299527168 | bytes 71304256 | tf_op jit(solution)/shard_map/sij,sif->sjf/dot_general | solution.py:45
  96.4 35.6 %copy.13 = f32[544,128,128]{2,1,0:T(8,128)} copy(f32[544,128,128]{1,2,0:T(8,128)} %fusion.6) | data formatting | bytes 71303168 | tf_op jit(solution)/shard_map/sij,sif->sjf/dot_general | solution.py:45
  132.1 3.4 broadcast_in_dim.36
  135.4 106.5 %scatter_fusion = f32[96,128,128]{2,1,0:T(8,128)} fusion(f32[96,128,128]{2,1,0:T(8,128)} %broadcast_in_dim.36, s32[544]{0:T(1024)S(1)} %get-tuple-element.7, f32[544,128,128]{2,1,0:T(8,128)} %copy.13), kind=kCustom, calls=%fused_computation.1 | custom fusion | flops 8912896 | bytes 106956928 | tf_op jit(solution)/shard_map/scatter-add | solution.py:57
  241.9 5.5 %fusion.33 = (f32[32,128,128]{2,1,0:T(8,128)}, f32[32,128,128]{2,1,0:T(8,128)}, f32[32,128,128]{2,1,0:T(8,128)S(1)}) fusion(f32[96,128,128]{2,1,0:T(8,128)} %scatter_fusion), kind=kLoop, calls=%fused_computation.66 | loop fusion | bytes 12582912 | tf_op jit(solution)/shard_map/slice | solution.py:14
  247.5 1.3 collective-permute-start
  248.8 2.8 collective-permute-start.1
  251.6 3.6 convolution_bitcast_fusion
  255.3 0.0 reduce-scatter.2.cloned.1.call-start
  255.3 84.6 %collective-permute-done = f32[1,4096,128]{2,1,0:T(8,128)} collective-permute-done((f32[1,4096,128]{2,1,0:T(8,128)}, f32[1,4096,128]{2,1,0:T(8,128)}, u32[]{:S(2)}, u32[]{:S(2)}) %collective-permute-start) | collective-permute-done | bytes 2097184 | tf_op jit(solution)/shard_map/ppermute | solution.py:17
  339.9 2.6 collective-permute-done.1
  342.5 2.6 fusion.13
  345.1 4.5 fusion.34
  349.6 38.6 %all-reduce.2.cloned.1.call-done = f32[512,128]{0,1:T(8,128)} async-done(((f32[512,128]{0,1:T(8,128)}), f32[512,128]{0,1:T(8,128)}) %all-reduce.2.cloned.1.call-update) | async-done | bytes 262160 | tf_op jit(solution)/shard_map/psum | solution.py:73
  388.2 1.8 copy.14
  390.0 80.7 %reduce-scatter.2.cloned.1.call-done = f32[4096,128]{1,0:T(8,128)} async-done(((f32[4096,512]{1,0:T(8,128)}), f32[4096,128]{1,0:T(8,128)}) %reduce-scatter.2.cloned.1.call-update) | async-done | bytes 2097168 | tf_op jit(solution)/shard_map/reduce_scatter | solution.py:64
  470.7 2.7 convert_element_type.11
  (16 shorter events, 0.1 us)
Async XLA Ops:
  7.2 337.9 %copy-start = (bf16[512,128]{1,0:T(8,128)(2,1)S(1)}, bf16[512,128]{1,0:T(8,128)(2,1)}, u32[]{:S(2)}) copy-start(bf16[512,128]{1,0:T(8,128)(2,1)} %param.11) | copy-start | bytes 393220
  7.2 4.6 copy-start.2
  7.2 4.6 copy-start.3
  7.2 44.4 %all-gather.3.cloned.1.call-start = ((), (), s32[]{:S(2)}) async-start(), calls=%async_computation.1 | async-start | bytes 5242880 | tf_op jit(solution)/shard_map/all_gather | solution.py:35
  10.3 241.3 %all-gather.5.cloned.1.call-start = ((), (), s32[]{:S(2)}) async-start(), calls=%async_computation.3 | async-start | bytes 5242880 | tf_op jit(solution)/shard_map/all_gather | solution.py:68
  11.1 377.2 %all-reduce.2.cloned.1.call-start = ((), (), s32[]{:S(2)}) async-start(), calls=%async_computation.4 | async-start | bytes 524288 | tf_op jit(solution)/shard_map/psum | solution.py:73
  241.9 9.7 %copy-start.1 = (bf16[4096,128]{1,0:T(8,128)(2,1)S(1)}, bf16[4096,128]{1,0:T(8,128)(2,1)}, u32[]{:S(2)}) copy-start(bf16[4096,128]{1,0:T(8,128)(2,1)} %convert_multiply_fusion) | copy-start | bytes 3145732
  247.5 92.4 %collective-permute-start = (f32[1,4096,128]{2,1,0:T(8,128)}, f32[1,4096,128]{2,1,0:T(8,128)}, u32[]{:S(2)}, u32[]{:S(2)}) collective-permute-start(f32[1,4096,128]{2,1,0:T(8,128)} %bitcast.6), channel_id=1, source_target_pairs={{0,16},{16,32},{32,48},{48,64},{64,80},{80,96},{96,112},{112,0},{1... | collective-permute-start | bytes 6291464 | tf_op jit(solution)/shard_map/ppermute | solution.py:17
  248.8 93.7 %collective-permute-start.1 = (f32[1,4096,128]{2,1,0:T(8,128)}, f32[1,4096,128]{2,1,0:T(8,128)}, u32[]{:S(2)}, u32[]{:S(2)}) collective-permute-start(f32[1,4096,128]{2,1,0:T(8,128)} %bitcast.9), channel_id=1, source_target_pairs={{16,0},{32,16},{48,32},{64,48},{80,64},{96,80},{112,96},{0,112},{1... | collective-permute-start | bytes 6291464 | tf_op jit(solution)/shard_map/ppermute | solution.py:19
  255.3 215.4 %reduce-scatter.2.cloned.1.call-start = ((), (), s32[]{:S(2)}) async-start(), calls=%async_computation.2 | async-start | bytes 10485760 | tf_op jit(solution)/shard_map/reduce_scatter | solution.py:64
Sparse Core Ops, SparseCore 0:
  10.4 41.1 all-gather.2
  53.2 51.1 all-gather.4
  255.4 132.7 all-reduce.1
  390.7 79.9 reduce-scatter.1
where the time goes:
time: 483 us; the launch traced here: 480 us
  waiting for transfers between devices  247 us (51%)
  other arithmetic  115 us (24%)
  local copies, waits for them, and re-layouts  64.2 us (13%)
  matrix products  35.1 us (7%)
  between operations  14.5 us (3%)
    scatter-add x1, other arithmetic, local(): buffer = jax.ops.segment_sum(contrib, segment, num_segments=3 * col_blocks)  106 us
    ppermute x1, waiting for transfers between devices, with_halo(): lax.ppermute(tail, axis, [(i, (i + 1) % count) for i in range(count)])  84.6 us
    reduce_scatter x1, waiting for transfers between devices, local(): lax.psum_scatter(partial_terms, 'depth', scatter_dimension=1, tiled=True)  80.7 us
    all_gather x1, waiting for transfers between devices, local(): stripe_grad = lax.all_gather(out_masked, 'col', axis=0, tiled=True)  39.7 us
    psum x1, waiting for transfers between devices, local(): grad_weight = lax.psum(weight_terms, ('row', 'col'))  38.6 us
    dot_general x1, local copies, waits for them, and re-layouts, local(): jnp.einsum('sij,sif->sjf', tile_values[0, 0], picked, preferred_element_t...  35.6 us
    dot_general x1, matrix products, local(): jnp.einsum('sij,sif->sjf', tile_values[0, 0], picked, preferred_element_t...  27 us
    gather x1, local copies, waits for them, and re-layouts, local(): picked = jnp.take(stripe_grad, source, axis=0)  17.8 us
  transfers between devices with their start and end apart: 6, of which 5 were waited for; matrix products, arithmetic and copies ran while one was open for 43% of the time, Pallas kernels for 0%

commit v1 on v0

v1 whole, which is shorter than its diff:
```python
import jax
import jax.numpy as jnp
from jax import lax
from jax.experimental import pallas as pl
from jax.experimental.pallas import tpu as pltpu
from jax.sharding import PartitionSpec as P

BW = 8
RB = 128
NBLK = 1024
T = 128
QUADS = 8
SLOTS = 5
RC = ("row", "col")
RD = ("row", "depth")
bf16 = jnp.bfloat16
f32 = jnp.float32


def ring(n, shift):
    return [(i, (i + shift) % n) for i in range(n)]


def flip(bit):
    return [(i, i ^ bit) for i in range(4)]


def params(mib):
    return pltpu.CompilerParams(vmem_limit_bytes=mib << 20)


SMEM = pl.BlockSpec(memory_space=pltpu.SMEM)
VMEM = pl.BlockSpec(memory_space=pltpu.VMEM)


def densify_kernel(inv, *refs):
    out = refs[-1]
    q = pl.program_id(0)
    for k in range(SLOTS * 4):
        slot, e = k // 4, k % 4
        tile = refs[k][0, 0, 0]
        live = inv[q * (SLOTS * 4) + k] >= 0
        turned = jnp.where(live, tile.T, jnp.zeros((T, T), bf16))
        out[0, slot * T:(slot + 1) * T, e * T:(e + 1) * T] = turned


def densify(inv, tile_values):
    def spec(k):
        return pl.BlockSpec(
            (1, 1, 1, T, T), lambda q, inv: (0, 0, jnp.maximum(inv[q * (SLOTS * 4) + k], 0), 0, 0)
        )

    return pl.pallas_call(
        densify_kernel,
        grid_spec=pltpu.PrefetchScalarGridSpec(
            num_scalar_prefetch=1,
            grid=(QUADS,),
            in_specs=[spec(k) for k in range(SLOTS * 4)],
            out_specs=pl.BlockSpec((1, SLOTS * T, 4 * T), lambda q, inv: (q, 0, 0)),
        ),
        out_shape=jax.ShapeDtypeStruct((QUADS, SLOTS * T, 4 * T), bf16),
        compiler_params=params(24),
        cost_estimate=pl.CostEstimate(flops=0, bytes_accessed=10 << 20, transcendentals=0),
        name="densify",
    )(inv, *([tile_values] * (SLOTS * 4)))


def tiles_kernel(band, a0, a1, a2, b0, b1, b2, inner, edge, low, high, acc):
    acc[...] = jnp.zeros_like(acc)
    for q in range(QUADS):
        rows = slice(q * T, (q + 1) * T)
        later = slice((QUADS + q) * T, (QUADS + q + 1) * T)
        sides = []
        for own, zed, pair in ((a0, a1, a2), (b0, b1, b2)):
            sides.append(jnp.concatenate([own[rows, :], pair[rows, :], zed[rows, :], pair[later, :]], axis=0))
        acc[q * T:(q + SLOTS) * T, :] += jnp.dot(
            band[q], jnp.concatenate(sides, axis=1), preferred_element_type=f32
        )
    low[...] = acc[0:2 * T, :].astype(bf16)
    high[...] = acc[10 * T:12 * T, :].astype(bf16)
    inner[...] = acc[4 * T:8 * T, :].astype(bf16)
    edge[0:2 * T, :] = acc[2 * T:4 * T, :]
    edge[2 * T:4 * T, :] = acc[8 * T:10 * T, :]


def tiles(band, first, second):
    return pl.pallas_call(
        tiles_kernel,
        in_specs=[VMEM] * 7,
        out_specs=[VMEM] * 4,
        out_shape=[
            jax.ShapeDtypeStruct((4 * T, 2 * T), bf16),
            jax.ShapeDtypeStruct((4 * T, 2 * T), f32),
            jax.ShapeDtypeStruct((2 * T, 2 * T), bf16),
            jax.ShapeDtypeStruct((2 * T, 2 * T), bf16),
        ],
        scratch_shapes=[pltpu.VMEM((12 * T, 2 * T), f32)],
        compiler_params=params(24),
        cost_estimate=pl.CostEstimate(flops=2 * 8 * 640 * 512 * 256, bytes_accessed=8 << 20, transcendentals=0),
        name="tiles",
    )(band, *first, *second)


def times_weight(depth, spread, weight, out, turned):
    for at, s in enumerate((0, 1, 3, 2)):
        src = pl.ds(pl.multiple_of(((depth[0] - s + 4) % 4) * T, T), T)
        turned[:, at * T:(at + 1) * T] = weight[:, src]
    got = lax.dot_general(spread, turned[...], (((1,), (1,)), ((), ())), preferred_element_type=f32).astype(bf16)
    for t in range(4):
        out[t] = got[:, t * T:(t + 1) * T]


def inner_kernel(depth, xa, xb, weight, out, turned):
    times_weight(depth, jnp.concatenate([xa[...], xb[...]], axis=1), weight, out, turned)


def edge_kernel(depth, xa, xb, na, nb, pa, pb, weight, out, turned):
    first, second = slice(0, T), slice(T, 2 * T)
    parts = (
        (xa, first, na, second, pb, first),
        (xa, second, nb, second, pa, first),
        (xb, first, na, first, pb, second),
        (xb, second, nb, first, pa, second),
    )
    chunks = []
    for x, at, n, n_at, p, p_at in parts:
        chunks.append(
            jnp.concatenate(
                [
                    (x[0:2 * T, at] + p[:, p_at].astype(f32)).astype(bf16),
                    (x[2 * T:4 * T, at] + n[:, n_at].astype(f32)).astype(bf16),
                ],
                axis=0,
            )
        )
    times_weight(depth, jnp.concatenate(chunks, axis=1), weight, out, turned)


def weighted(kernel, name, depth, arrays):
    return pl.pallas_call(
        kernel,
        in_specs=[SMEM] + [VMEM] * len(arrays),
        out_specs=VMEM,
        out_shape=jax.ShapeDtypeStruct((4, 4 * T, T), bf16),
        scratch_shapes=[pltpu.VMEM((4 * T, 4 * T), bf16)],
        compiler_params=params(16),
        cost_estimate=pl.CostEstimate(flops=2 * 512 * 512 * 512, bytes_accessed=3 << 20, transcendentals=0),
        name=name,
    )(depth, *arrays)


def outer_kernel(depth, agg, m0, m1, m2, m3, out, turned):
    for s, m in enumerate((m0, m1, m2, m3)):
        dst = pl.ds(pl.multiple_of(((depth[0] - s + 4) % 4) * T, T), T)
        turned[:, dst] = m[...]
    for a in range(4):
        got = lax.dot_general(
            agg[a], turned[...], (((0,), (0,)), ((), ())), preferred_element_type=f32
        ).astype(bf16)
        for t in range(4):
            out[a * 8:(a + 1) * 8, t] = got[:, t * T:(t + 1) * T].reshape(8, 16, T)


def outer(depth, agg, ms):
    return pl.pallas_call(
        outer_kernel,
        in_specs=[SMEM] + [VMEM] * 5,
        out_specs=VMEM,
        out_shape=jax.ShapeDtypeStruct((32, 4, 16, T), bf16),
        scratch_shapes=[pltpu.VMEM((8 * T, 4 * T), bf16)],
        compiler_params=params(16),
        cost_estimate=pl.CostEstimate(flops=2 * 512 * 512 * 1024, bytes_accessed=3 << 20, transcendentals=0),
        name="outer",
    )(depth, agg, *ms)


def inverse_table(rows, cols, count, stripe, col, depth):
    slot_ids = jnp.arange(rows.shape[0], dtype=jnp.int32)
    shift = (cols - (stripe * RB + rows) + BW) % NBLK
    within = rows % 32
    quad = within // 4
    slot = (within + shift - col) // 4 - quad
    key = (quad * SLOTS + slot) * 4 + ((rows % 4) ^ col)
    key = jnp.where((slot_ids < count) & (rows // 32 == depth), key, -1)
    targets = jnp.arange(QUADS * SLOTS * 4, dtype=jnp.int32)
    return jnp.max(jnp.where(key[None, :] == targets[:, None], slot_ids[None, :], -1), axis=1)


def local(out_grad, relu_mask, aggregated, weight, tile_values, tile_rows, tile_cols, tile_count):
    stripe = lax.axis_index("row")
    col = lax.axis_index("col")
    depth = lax.axis_index("depth")
    depth1 = depth.reshape(1).astype(jnp.int32)

    def quarter(array, t):
        return lax.dynamic_slice_in_dim(array, ((depth + t) % 4) * 1024, 1024, axis=0)

    def masked(t):
        return jnp.where(quarter(relu_mask, t) != 0, quarter(out_grad, t), jnp.zeros((), bf16))

    def from_depth(array, t):
        return lax.ppermute(array, "depth", ring(4, t))

    rows = [masked(0)] + [from_depth(masked(t), t) for t in (1, 2, 3)]
    whole_weight = lax.all_gather(weight, "depth", axis=1, tiled=True)

    inv = inverse_table(tile_rows[0, 0], tile_cols[0, 0], tile_count[0, 0], stripe, col, depth)
    band = densify(inv, tile_values)

    def spread_out(own):
        zed = lax.ppermute(own, "col", flip(2))
        pair = lax.ppermute(jnp.concatenate([own, zed], axis=0), "col", flip(1))
        return own, zed, pair

    chunks = {s: spread_out(rows[s]) for s in (0, 1, 3, 2)}
    inner_a, edge_a, low_a, high_a = tiles(band, chunks[0], chunks[1])
    next_a = lax.ppermute(low_a, RD, ring(32, -1))
    prev_a = lax.ppermute(high_a, RD, ring(32, 1))
    inner_b, edge_b, low_b, high_b = tiles(band, chunks[3], chunks[2])
    next_b = lax.ppermute(low_b, RD, ring(32, -1))
    prev_b = lax.ppermute(high_b, RD, ring(32, 1))

    inner = weighted(inner_kernel, "inner_rows", depth1, [inner_a, inner_b, whole_weight])
    inner = lax.all_to_all(inner, "depth", 0, 0)
    edge = weighted(
        edge_kernel, "edge_rows", depth1, [edge_a, edge_b, next_a, next_b, prev_a, prev_b, whole_weight]
    )
    edge = lax.all_to_all(edge, "depth", 0, 0)
    grad_input = jnp.concatenate([edge[:, :2 * T], inner, edge[:, 2 * T:]], axis=1).reshape(32 * T, T)

    late, _ = lax.optimization_barrier((aggregated, (rows[2], rows[3])))
    agg = lax.all_to_all(late.reshape(4, 8 * T, T), "depth", 0, 0)
    pieces = outer(depth1, agg, rows).reshape(128, 16, T)
    pieces = lax.all_to_all(pieces, ("row", "col", "depth"), 0, 0)
    piece = jnp.sum(pieces.astype(f32), axis=0)
    grad_weight = lax.all_to_all(jnp.broadcast_to(piece, (32, 16, T)), RC, 0, 0).reshape(4 * T, T)
    return grad_input, grad_weight


def solution(mesh):
    placed = (
        P(RC, "depth"),
        P(RC, "depth"),
        P(RC, "depth"),
        P(None, "depth"),
        P("row", "col", None, None, None),
        P("row", "col", None),
        P("row", "col", None),
        P("row", "col"),
    )
    return jax.shard_map(
        local,
        mesh=mesh,
        in_specs=placed,
        out_specs=(P(RC, "depth"), P(None, "depth")),
        check_vma=False,
    )
```

time: 483 us -> 139 us (0.29)
  waiting for transfers between devices: 247 us -> 40.7 us
  other arithmetic: 115 us -> 5.46 us
  local copies, waits for them, and re-layouts: 64.2 us -> 10.8 us
  starting transfers between devices: 4.29 us -> 53 us
  matrix products: 35.1 us -> 0 us
  blocking collectives: 0 us -> 14.8 us
  between operations: 14.5 us -> 1.56 us
  Pallas kernels: 0 us -> 10.9 us
    scatter-add x1 -> x0, other arithmetic: 106 us -> none  [local(): buffer = jax.ops.segment_sum(contrib, segment, num_segments=3 * col_blocks)]
    reduce_scatter x1 -> x0, waiting for transfers between devices: 80.7 us -> none  [local(): lax.psum_scatter(partial_terms, 'depth', scatter_dimension=1, tiled=True)]
    ppermute x2 -> x15, waiting for transfers between devices: 87.2 us -> 19.3 us  [the longest x4 9.45 us: spread_out(): zed = lax.ppermute(own, 'col', flip(2))]
    all_gather x2 -> x0, waiting for transfers between devices: 39.7 us -> none  [the longest x1 39.7 us: local(): stripe_grad = lax.all_gather(out_masked, 'col', axis=0, tiled=True)]
    psum x1 -> x0, waiting for transfers between devices: 38.6 us -> none  [local(): grad_weight = lax.psum(weight_terms, ('row', 'col'))]
    dot_general x1 -> x0, local copies, waits for them, and re-layouts: 35.6 us -> none  [local(): jnp.einsum('sij,sif->sjf', tile_values[0, 0], picked, preferred_element_t...]
    dot_general x3 -> x0, matrix products: 35.1 us -> none  [the longest x1 27 us: local(): jnp.einsum('sij,sif->sjf', tile_values[0, 0], picked, preferred_element_t...]
    ppermute x2 -> x15, starting transfers between devices: 4.14 us -> 30.6 us  [the longest x4 12.9 us: spread_out(): zed = lax.ppermute(own, 'col', flip(2))]
  transfers between devices with their start and end apart: 6 -> 20, of which waited for: 5 -> 9; matrix products, arithmetic and copies ran while one was open for 43% -> 2% of each run, Pallas kernels for 0% -> 8%
where the time goes in v1:
time: 139 us; the launch traced here: 137 us
  starting transfers between devices  53 us (38%)
  waiting for transfers between devices  40.7 us (29%)
  blocking collectives  14.8 us (11%)
  Pallas kernels  10.9 us (8%)
  local copies, waits for them, and re-layouts  10.8 us (8%)
  other arithmetic  5.46 us (4%)
  between operations  1.56 us (1%)
    all_gather x1, blocking collectives, local(): whole_weight = lax.all_gather(weight, 'depth', axis=1, tiled=True)  14.8 us
    ppermute x4, starting transfers between devices, spread_out(): zed = lax.ppermute(own, 'col', flip(2))  12.9 us
    unnamed x23, local copies, waits for them, and re-layouts  10.1 us
    ppermute x4, waiting for transfers between devices, spread_out(): zed = lax.ppermute(own, 'col', flip(2))  9.45 us
    all_to_all x1, waiting for transfers between devices, local(): edge = lax.all_to_all(edge, 'depth', 0, 0)  7.9 us
    all_to_all x1, waiting for transfers between devices, local(): lax.all_to_all(jnp.broadcast_to(piece, (32, 16, T)), RC, 0, 0)  6.79 us
    all_to_all x1, waiting for transfers between devices, local(): inner = lax.all_to_all(inner, 'depth', 0, 0)  6.7 us
    ppermute x1, starting transfers between devices, local(): next_a = lax.ppermute(low_a, RD, ring(32, -1))  6.24 us
  transfers between devices with their start and end apart: 20, of which 9 were waited for; matrix products, arithmetic and copies ran while one was open for 2% of the time, Pallas kernels for 8%

profile of v1, /device:TPU:0, one launch (start us, length us, event | category | flops | bytes accessed | tf_op | source)
XLA Modules:
  0.0 137.4 jit_solution(3444211613187307931)
XLA Ops:
  0.7 2.1 %fusion.3 = (bf16[1024,128]{1,0:T(8,128)(2,1)S(1)}, bf16[1024,128]{1,0:T(8,128)(2,1)S(1)}, bf16[1024,128]{1,0:T(8,128)(2,1)S(1)}, bf16[1024,128]{1,0:T(8,128)(2,1)S(1)}) fusion(s32[4096,128]{1,0:T(8,128)} %param.9, s32[]{:T(128)S(6)} %select_n.135, bf16[4096,128]{1,0:T(8,128)(2,1)} %param.8, s32[]{:T(128)S(6)} %select_n.129, s32[]{:T(128)S(6)} %select_n.126, ...), kind=kLoop, calls=%fused_computation.13 | loop fusion | flops 1048576 | bytes 4194320 | tf_op jit(solution)/shard_map/jit(_where)/select_n | solution.py:199
  2.8 3.4 %collective-permute-start.8 = (bf16[1024,128]{1,0:T(8,128)(2,1)S(1)}, bf16[1024,128]{1,0:T(8,128)(2,1)S(1)}, u32[]{:S(2)}, u32[]{:S(2)}) collective-permute-start(bf16[1024,128]{1,0:T(8,128)(2,1)S(1)} %get-tuple-element.20), channel_id=1, source_target_pairs={{0,2},{1,3},{2,0},{3,1},{4,6},{5,7},{6,4},{7,5},{8,10},{9,11},{10,... | collective-permute-start | bytes 786440 | tf_op jit(solution)/shard_map/ppermute | solution.py:202
  7.2 3.9 %collective-permute-start = (bf16[1024,128]{1,0:T(8,128)(2,1)S(1)}, bf16[1024,128]{1,0:T(8,128)(2,1)S(1)}, u32[]{:S(2)}, u32[]{:S(2)}) collective-permute-start(bf16[1024,128]{1,0:T(8,128)(2,1)S(1)} %get-tuple-element.22.a0.m0), channel_id=1, source_target_pairs={{0,8},{4,12},{8,0},{12,4},{1,9},{5,13},{9,1},{13,5},{2,10},{6,14},... | collective-permute-start | bytes 786440 | tf_op jit(solution)/shard_map/ppermute | solution.py:211
  12.5 5.1 %collective-permute-start.9 = (bf16[1024,128]{1,0:T(8,128)(2,1)S(1)}, bf16[1024,128]{1,0:T(8,128)(2,1)S(1)}, u32[]{:S(2)}, u32[]{:S(2)}) collective-permute-start(bf16[1024,128]{1,0:T(8,128)(2,1)S(1)} %collective-permute-done.8.b0.m2), channel_id=1, source_target_pairs={{0,8},{4,12},{8,0},{12,4},{1,9},{5,13},{9,1},{13,5},{2,10},{6,14},... | collective-permute-start | bytes 786440 | tf_op jit(solution)/shard_map/ppermute | solution.py:211
  18.5 3.9 %collective-permute-start.6 = (bf16[1024,128]{1,0:T(8,128)(2,1)S(1)}, bf16[1024,128]{1,0:T(8,128)(2,1)S(1)}, u32[]{:S(2)}, u32[]{:S(2)}) collective-permute-start(bf16[1024,128]{1,0:T(8,128)(2,1)S(1)} %collective-permute-done.5.a0.m3), channel_id=1, source_target_pairs={{0,8},{4,12},{8,0},{12,4},{1,9},{5,13},{9,1},{13,5},{2,10},{6,14},... | collective-permute-start | bytes 786440 | tf_op jit(solution)/shard_map/ppermute | solution.py:211
  23.2 3.9 %all-to-all-start.2 = ((bf16[4,1024,128]{2,1,0:T(8,128)(2,1)}), bf16[4,1024,128]{2,1,0:T(8,128)(2,1)S(1)}, u32[]{:S(2)}, u32[]{:S(2)}) async-start(bf16[4,1024,128]{2,1,0:T(8,128)(2,1)} %bitcast.7), calls=%async_computation.2 | async-start | bytes 2097152 | tf_op jit(solution)/shard_map/all_to_all | solution.py:232
  28.2 8.9 %collective-permute-done.3.b1 = bf16[1024,128]{1,0:T(8,128)(2,1)S(1)} collective-permute-done((bf16[1024,128]{1,0:T(8,128)(2,1)S(1)}, bf16[1024,128]{1,0:T(8,128)(2,1)S(1)}, u32[]{:S(2)}, u32[]{:S(2)}) %collective-permute-start.3) | collective-permute-done | bytes 262176 | tf_op jit(solution)/shard_map/ppermute | solution.py:211
  37.4 6.1 %copy-done = bf16[1,1,544,128,128]{4,3,2,1,0:T(8,128)(2,1)S(1)} copy-done((bf16[1,1,544,128,128]{4,3,2,1,0:T(8,128)(2,1)S(1)}, bf16[1,1,544,128,128]{4,3,2,1,0:T(8,128)(2,1)}, u32[]{:S(2)}) %copy-start) | copy-done | bytes 17825816
  43.5 2.5 %densify.1.band = bf16[8,640,512]{2,1,0:T(8,128)(2,1)S(1)} custom-call(s32[160]{0:T(256)S(1)} %select_reduce_fusion.inv, bf16[1,1,544,128,128]{4,3,2,1,0:T(8,128)(2,1)S(1)} %copy-done, bf16[1,1,544,128,128]{4,3,2,1,0:T(8,128)(2,1)S(1)} %copy-done, bf16[1,1,544,128,128]{4,3,2,1,0:T(8,128)(2,1)S(1)} %copy-done, bf16[1,1,544,128,128]{4,3,2,1,0:T(8,128)(2,1)S(1)} %copy-done, ...), custom_call_target="tpu_custom_call" | custom-call | bytes 10485760 | tf_op jit(solution)/shard_map/densify/pallas_call | solution.py:53
  46.0 14.8 %all_gather.3.weight = bf16[512,512]{1,0:T(8,128)(2,1)S(1)} all-gather(bf16[512,128]{1,0:T(8,128)(2,1)S(1)} %copy-done.8), channel_id=1, replica_groups=mesh['row'=8,'col'=4,'depth'=4] {'depth'}, dimensions={1}, use_global_device_ids=true | all-gather | bytes 655360 | tf_op jit(solution)/shard_map/all_gather | solution.py:205
  63.8 2.6 %tiles.2 = (bf16[512,256]{1,0:T(8,128)(2,1)S(1)}, f32[512,256]{1,0:T(8,128)S(1)}, bf16[256,256]{1,0:T(8,128)(2,1)S(1)}, bf16[256,256]{1,0:T(8,128)(2,1)S(1)}) custom-call(bf16[8,640,512]{2,1,0:T(8,128)(2,1)S(1)} %densify.1.band, bf16[1024,128]{1,0:T(8,128)(2,1)S(1)} %get-tuple-element.22.a0.m0, bf16[1024,128]{1,0:T(8,128)(2,1)S(1)} %collective-permute-done.a1, ...), custom_call_target="tpu_custom_call" | custom-call | flops 1342177280 | bytes 8388608 | tf_op jit(solution)/shard_map/tiles/pallas_call | solution.py:87
  68.5 4.1 %all-to-all-start.1 = ((bf16[4,512,128]{2,1,0:T(8,128)(2,1)}), bf16[4,512,128]{2,1,0:T(8,128)(2,1)}, u32[]{:S(2)}, u32[]{:S(2)}) async-start(bf16[4,512,128]{2,1,0:T(8,128)(2,1)} %inner_rows.1), calls=%async_computation.1 | async-start | bytes 1048576 | tf_op jit(solution)/shard_map/all_to_all | solution.py:224
  72.6 1.8 %outer.1 = bf16[32,4,16,128]{3,2,1,0:T(8,128)(2,1)} custom-call(s32[1]{0:T(128)} %bitcast.depth, bf16[4,1024,128]{2,1,0:T(8,128)(2,1)S(1)} %all-to-all-done.2.agg, bf16[1024,128]{1,0:T(8,128)(2,1)S(1)} %get-tuple-element.22.a0.m0, bf16[1024,128]{1,0:T(8,128)(2,1)S(1)} %collective-permute-done.2.b0.m1, bf16[1024,128]{1,0:T(8,128)(2,1)S(1)} %collective-permute-done.8.b0.m2, ...), custom_call_target="tpu_custom_call" | custom-call | flops 536870912 | bytes 3145728 | tf_op jit(solution)/shard_map/outer/pallas_call | solution.py:165
  74.4 6.7 %all-to-all-done.1 = bf16[4,512,128]{2,1,0:T(8,128)(2,1)} async-done(((bf16[4,512,128]{2,1,0:T(8,128)(2,1)}), bf16[4,512,128]{2,1,0:T(8,128)(2,1)}, u32[]{:S(2)}, u32[]{:S(2)}) %all-to-all-start.1) | async-done | bytes 524320 | tf_op jit(solution)/shard_map/all_to_all | solution.py:224
  81.1 6.1 %all-to-all-start.3 = ((bf16[128,16,128]{2,1,0:T(8,128)(2,1)}), bf16[128,16,128]{2,1,0:T(8,128)(2,1)S(1)}, u32[]{:S(2)}, u32[]{:S(2)}) async-start(bf16[128,16,128]{2,1,0:T(8,128)(2,1)} %bitcast.4), calls=%async_computation.3 | async-start | bytes 1048576 | tf_op jit(solution)/shard_map/all_to_all | solution.py:234
  87.2 5.6 %collective-permute-start.12 = (bf16[256,256]{1,0:T(8,128)(2,1)S(1)}, bf16[256,256]{1,0:T(8,128)(2,1)S(1)}, u32[]{:S(2)}, u32[]{:S(2)}) collective-permute-start(bf16[256,256]{1,0:T(8,128)(2,1)S(1)} %copy-done.6), channel_id=1, source_target_pairs={{0,115},{1,0},{2,1},{3,2},{16,3},{17,16},{18,17},{19,18},{32,19},{... | collective-permute-start | bytes 393224 | tf_op jit(solution)/shard_map/ppermute | solution.py:220
  92.8 6.2 %collective-permute-start.11 = (bf16[256,256]{1,0:T(8,128)(2,1)}, bf16[256,256]{1,0:T(8,128)(2,1)S(1)}, u32[]{:S(2)}, u32[]{:S(2)}) collective-permute-start(bf16[256,256]{1,0:T(8,128)(2,1)} %copy-done.7), channel_id=1, source_target_pairs={{0,115},{1,0},{2,1},{3,2},{16,3},{17,16},{18,17},{19,18},{32,19},{... | collective-permute-start | bytes 393224 | tf_op jit(solution)/shard_map/ppermute | solution.py:217
  99.1 3.2 %collective-permute-done.14.pb = bf16[256,256]{1,0:T(8,128)(2,1)S(1)} collective-permute-done((bf16[256,256]{1,0:T(8,128)(2,1)S(1)}, bf16[256,256]{1,0:T(8,128)(2,1)S(1)}, u32[]{:S(2)}, u32[]{:S(2)}) %collective-permute-start.14) | collective-permute-done | bytes 131104 | tf_op jit(solution)/shard_map/ppermute | solution.py:221
  102.3 5.9 %collective-permute-done.13.pa = bf16[256,256]{1,0:T(8,128)(2,1)S(1)} collective-permute-done((bf16[256,256]{1,0:T(8,128)(2,1)S(1)}, bf16[256,256]{1,0:T(8,128)(2,1)S(1)}, u32[]{:S(2)}, u32[]{:S(2)}) %collective-permute-start.13) | collective-permute-done | bytes 131104 | tf_op jit(solution)/shard_map/ppermute | solution.py:218
  110.6 3.5 %all-to-all-start = ((bf16[4,512,128]{2,1,0:T(8,128)(2,1)}), bf16[4,512,128]{2,1,0:T(8,128)(2,1)S(1)}, u32[]{:S(2)}, u32[]{:S(2)}) async-start(bf16[4,512,128]{2,1,0:T(8,128)(2,1)} %edge_rows.1), calls=%async_computation | async-start | bytes 1048576 | tf_op jit(solution)/shard_map/all_to_all | solution.py:228
  114.2 7.9 %all-to-all-done = bf16[4,512,128]{2,1,0:T(8,128)(2,1)S(1)} async-done(((bf16[4,512,128]{2,1,0:T(8,128)(2,1)}), bf16[4,512,128]{2,1,0:T(8,128)(2,1)S(1)}, u32[]{:S(2)}, u32[]{:S(2)}) %all-to-all-start) | async-done | bytes 524320 | tf_op jit(solution)/shard_map/all_to_all | solution.py:228
  122.8 4.9 %all-to-all-start.4 = ((f32[32,16,128]{2,1,0:T(8,128)}), f32[32,16,128]{2,1,0:T(8,128)S(1)}, u32[]{:S(2)}, u32[]{:S(2)}) async-start(f32[32,16,128]{2,1,0:T(8,128)} %broadcast_in_dim.30), calls=%async_computation.4 | async-start | bytes 524288 | tf_op jit(solution)/shard_map/all_to_all | solution.py:236
  127.8 2.1 %pad_maximum_fusion = bf16[4,1024,128]{2,1,0:T(8,128)(2,1)} fusion(bf16[4,256,128]{2,1,0:T(8,128)(2,1)S(1)} %get-tuple-element.25, bf16[4,512,128]{2,1,0:T(8,128)(2,1)} %all-to-all-done.1, bf16[4,256,128]{2,1,0:T(8,128)(2,1)S(1)} %get-tuple-element.24), kind=kLoop, calls=%fused_computation | loop fusion | flops 3145728 | bytes 2097152 | tf_op jit(solution)/shard_map/concatenate | solution.py:229
  129.9 6.8 %all-to-all-done.4 = f32[32,16,128]{2,1,0:T(8,128)S(1)} async-done(((f32[32,16,128]{2,1,0:T(8,128)}), f32[32,16,128]{2,1,0:T(8,128)S(1)}, u32[]{:S(2)}, u32[]{:S(2)}) %all-to-all-start.4) | async-done | bytes 262176 | tf_op jit(solution)/shard_map/all_to_all | solution.py:236
  (59 shorter events, 14.0 us)
Async XLA Ops:
  0.7 16.9 %copy-start.9 = (s32[1,1,544]{2,1,0:T(1,128)S(1)}, s32[1,1,544]{2,1,0:T(1,128)}, u32[]{:S(2)}) copy-start(s32[1,1,544]{2,1,0:T(1,128)} %param.13) | copy-start | bytes 6532
  0.7 16.9 %copy-start.10 = (s32[1,1,544]{2,1,0:T(1,128)S(1)}, s32[1,1,544]{2,1,0:T(1,128)}, u32[]{:S(2)}) copy-start(s32[1,1,544]{2,1,0:T(1,128)} %param.14) | copy-start | bytes 6532
  2.8 9.7 %collective-permute-start.8 = (bf16[1024,128]{1,0:T(8,128)(2,1)S(1)}, bf16[1024,128]{1,0:T(8,128)(2,1)S(1)}, u32[]{:S(2)}, u32[]{:S(2)}) collective-permute-start(bf16[1024,128]{1,0:T(8,128)(2,1)S(1)} %get-tuple-element.20), channel_id=1, source_target_pairs={{0,2},{1,3},{2,0},{3,1},{4,6},{5,7},{6,4},{7,5},{8,10},{9,11},{10,... | collective-permute-start | bytes 786440 | tf_op jit(solution)/shard_map/ppermute | solution.py:202
  6.2 12.4 %collective-permute-start.5 = (bf16[1024,128]{1,0:T(8,128)(2,1)S(1)}, bf16[1024,128]{1,0:T(8,128)(2,1)S(1)}, u32[]{:S(2)}, u32[]{:S(2)}) collective-permute-start(bf16[1024,128]{1,0:T(8,128)(2,1)S(1)} %get-tuple-element.23), channel_id=1, source_target_pairs={{0,3},{1,0},{2,1},{3,2},{4,7},{5,4},{6,5},{7,6},{8,11},{9,8},{10,9... | collective-permute-start | bytes 786440 | tf_op jit(solution)/shard_map/ppermute | solution.py:202
  7.2 15.2 %collective-permute-start = (bf16[1024,128]{1,0:T(8,128)(2,1)S(1)}, bf16[1024,128]{1,0:T(8,128)(2,1)S(1)}, u32[]{:S(2)}, u32[]{:S(2)}) collective-permute-start(bf16[1024,128]{1,0:T(8,128)(2,1)S(1)} %get-tuple-element.22.a0.m0), channel_id=1, source_target_pairs={{0,8},{4,12},{8,0},{12,4},{1,9},{5,13},{9,1},{13,5},{2,10},{6,14},... | collective-permute-start | bytes 786440 | tf_op jit(solution)/shard_map/ppermute | solution.py:211
  11.1 16.0 %collective-permute-start.2 = (bf16[1024,128]{1,0:T(8,128)(2,1)S(1)}, bf16[1024,128]{1,0:T(8,128)(2,1)S(1)}, u32[]{:S(2)}, u32[]{:S(2)}) collective-permute-start(bf16[1024,128]{1,0:T(8,128)(2,1)S(1)} %get-tuple-element.21), channel_id=1, source_target_pairs={{0,1},{1,2},{2,3},{3,0},{4,5},{5,6},{6,7},{7,4},{8,9},{9,10},{10,1... | collective-permute-start | bytes 786440 | tf_op jit(solution)/shard_map/ppermute | solution.py:202
  12.5 14.7 %collective-permute-start.9 = (bf16[1024,128]{1,0:T(8,128)(2,1)S(1)}, bf16[1024,128]{1,0:T(8,128)(2,1)S(1)}, u32[]{:S(2)}, u32[]{:S(2)}) collective-permute-start(bf16[1024,128]{1,0:T(8,128)(2,1)S(1)} %collective-permute-done.8.b0.m2), channel_id=1, source_target_pairs={{0,8},{4,12},{8,0},{12,4},{1,9},{5,13},{9,1},{13,5},{2,10},{6,14},... | collective-permute-start | bytes 786440 | tf_op jit(solution)/shard_map/ppermute | solution.py:211
  18.5 9.6 %collective-permute-start.6 = (bf16[1024,128]{1,0:T(8,128)(2,1)S(1)}, bf16[1024,128]{1,0:T(8,128)(2,1)S(1)}, u32[]{:S(2)}, u32[]{:S(2)}) collective-permute-start(bf16[1024,128]{1,0:T(8,128)(2,1)S(1)} %collective-permute-done.5.a0.m3), channel_id=1, source_target_pairs={{0,8},{4,12},{8,0},{12,4},{1,9},{5,13},{9,1},{13,5},{2,10},{6,14},... | collective-permute-start | bytes 786440 | tf_op jit(solution)/shard_map/ppermute | solution.py:211
  23.2 40.6 %collective-permute-start.1 = (bf16[2048,128]{1,0:T(8,128)(2,1)}, bf16[2048,128]{1,0:T(8,128)(2,1)}, u32[]{:S(2)}, u32[]{:S(2)}) collective-permute-start(bf16[2048,128]{1,0:T(8,128)(2,1)} %pad_maximum_fusion.1), channel_id=1, source_target_pairs={{0,4},{4,0},{8,12},{12,8},{1,5},{5,1},{9,13},{13,9},{2,6},{6,2},{1... | collective-permute-start | bytes 1572872 | tf_op jit(solution)/shard_map/ppermute | solution.py:212
  23.2 45.2 %all-to-all-start.2 = ((bf16[4,1024,128]{2,1,0:T(8,128)(2,1)}), bf16[4,1024,128]{2,1,0:T(8,128)(2,1)S(1)}, u32[]{:S(2)}, u32[]{:S(2)}) async-start(bf16[4,1024,128]{2,1,0:T(8,128)(2,1)} %bitcast.7), calls=%async_computation.2 | async-start | bytes 2097152 | tf_op jit(solution)/shard_map/all_to_all | solution.py:232
  27.1 9.9 %collective-permute-start.3 = (bf16[1024,128]{1,0:T(8,128)(2,1)S(1)}, bf16[1024,128]{1,0:T(8,128)(2,1)S(1)}, u32[]{:S(2)}, u32[]{:S(2)}) collective-permute-start(bf16[1024,128]{1,0:T(8,128)(2,1)S(1)} %collective-permute-done.2.b0.m1), channel_id=1, source_target_pairs={{0,8},{4,12},{8,0},{12,4},{1,9},{5,13},{9,1},{13,5},{2,10},{6,14},... | collective-permute-start | bytes 786440 | tf_op jit(solution)/shard_map/ppermute | solution.py:211
  27.3 33.5 %collective-permute-start.10 = (bf16[2048,128]{1,0:T(8,128)(2,1)S(1)}, bf16[2048,128]{1,0:T(8,128)(2,1)S(1)}, u32[]{:S(2)}, u32[]{:S(2)}) collective-permute-start(bf16[2048,128]{1,0:T(8,128)(2,1)S(1)} %pad_maximum_fusion.4), channel_id=1, source_target_pairs={{0,4},{4,0},{8,12},{12,8},{1,5},{5,1},{9,13},{13,9},{2,6},{6,2},{1... | collective-permute-start | bytes 1572872 | tf_op jit(solution)/shard_map/ppermute | solution.py:212
  28.1 32.7 %collective-permute-start.7 = (bf16[2048,128]{1,0:T(8,128)(2,1)S(1)}, bf16[2048,128]{1,0:T(8,128)(2,1)S(1)}, u32[]{:S(2)}, u32[]{:S(2)}) collective-permute-start(bf16[2048,128]{1,0:T(8,128)(2,1)S(1)} %pad_maximum_fusion.3), channel_id=1, source_target_pairs={{0,4},{4,0},{8,12},{12,8},{1,5},{5,1},{9,13},{13,9},{2,6},{6,2},{1... | collective-permute-start | bytes 1572872 | tf_op jit(solution)/shard_map/ppermute | solution.py:212
  37.1 26.7 %collective-permute-start.4 = (bf16[2048,128]{1,0:T(8,128)(2,1)S(1)}, bf16[2048,128]{1,0:T(8,128)(2,1)S(1)}, u32[]{:S(2)}, u32[]{:S(2)}) collective-permute-start(bf16[2048,128]{1,0:T(8,128)(2,1)S(1)} %pad_maximum_fusion.2), channel_id=1, source_target_pairs={{0,4},{4,0},{8,12},{12,8},{1,5},{5,1},{9,13},{13,9},{2,6},{6,2},{1... | collective-permute-start | bytes 1572872 | tf_op jit(solution)/shard_map/ppermute | solution.py:212
  68.5 12.6 %all-to-all-start.1 = ((bf16[4,512,128]{2,1,0:T(8,128)(2,1)}), bf16[4,512,128]{2,1,0:T(8,128)(2,1)}, u32[]{:S(2)}, u32[]{:S(2)}) async-start(bf16[4,512,128]{2,1,0:T(8,128)(2,1)} %inner_rows.1), calls=%async_computation.1 | async-start | bytes 1048576 | tf_op jit(solution)/shard_map/all_to_all | solution.py:224
  72.6 14.5 %copy-start.6 = (bf16[256,256]{1,0:T(8,128)(2,1)S(1)}, bf16[256,256]{1,0:T(8,128)(2,1)}, u32[]{:S(2)}) copy-start(bf16[256,256]{1,0:T(8,128)(2,1)} %copy-done.5) | copy-start | bytes 393220
  72.6 35.6 %copy-start.2 = (f32[512,256]{1,0:T(8,128)S(1)}, f32[512,256]{1,0:T(8,128)}, u32[]{:S(2)}) copy-start(f32[512,256]{1,0:T(8,128)} %copy-done.1) | copy-start | bytes 1572868
  81.1 29.5 %all-to-all-start.3 = ((bf16[128,16,128]{2,1,0:T(8,128)(2,1)}), bf16[128,16,128]{2,1,0:T(8,128)(2,1)S(1)}, u32[]{:S(2)}, u32[]{:S(2)}) async-start(bf16[128,16,128]{2,1,0:T(8,128)(2,1)} %bitcast.4), calls=%async_computation.3 | async-start | bytes 1048576 | tf_op jit(solution)/shard_map/all_to_all | solution.py:234
  87.2 11.9 %collective-permute-start.12 = (bf16[256,256]{1,0:T(8,128)(2,1)S(1)}, bf16[256,256]{1,0:T(8,128)(2,1)S(1)}, u32[]{:S(2)}, u32[]{:S(2)}) collective-permute-start(bf16[256,256]{1,0:T(8,128)(2,1)S(1)} %copy-done.6), channel_id=1, source_target_pairs={{0,115},{1,0},{2,1},{3,2},{16,3},{17,16},{18,17},{19,18},{32,19},{... | collective-permute-start | bytes 393224 | tf_op jit(solution)/shard_map/ppermute | solution.py:220
  92.8 9.5 %collective-permute-start.14 = (bf16[256,256]{1,0:T(8,128)(2,1)S(1)}, bf16[256,256]{1,0:T(8,128)(2,1)S(1)}, u32[]{:S(2)}, u32[]{:S(2)}) collective-permute-start(bf16[256,256]{1,0:T(8,128)(2,1)S(1)} %get-tuple-element.16), channel_id=1, source_target_pairs={{0,1},{1,2},{2,3},{3,16},{16,17},{17,18},{18,19},{19,32},{32,33},{... | collective-permute-start | bytes 393224 | tf_op jit(solution)/shard_map/ppermute | solution.py:221
  92.8 9.5 %collective-permute-start.11 = (bf16[256,256]{1,0:T(8,128)(2,1)}, bf16[256,256]{1,0:T(8,128)(2,1)S(1)}, u32[]{:S(2)}, u32[]{:S(2)}) collective-permute-start(bf16[256,256]{1,0:T(8,128)(2,1)} %copy-done.7), channel_id=1, source_target_pairs={{0,115},{1,0},{2,1},{3,2},{16,3},{17,16},{18,17},{19,18},{32,19},{... | collective-permute-start | bytes 393224 | tf_op jit(solution)/shard_map/ppermute | solution.py:217
  99.0 9.2 %collective-permute-start.13 = (bf16[256,256]{1,0:T(8,128)(2,1)S(1)}, bf16[256,256]{1,0:T(8,128)(2,1)S(1)}, u32[]{:S(2)}, u32[]{:S(2)}) collective-permute-start(bf16[256,256]{1,0:T(8,128)(2,1)S(1)} %get-tuple-element.15), channel_id=1, source_target_pairs={{0,1},{1,2},{2,3},{3,16},{16,17},{17,18},{18,19},{19,32},{32,33},{... | collective-permute-start | bytes 393224 | tf_op jit(solution)/shard_map/ppermute | solution.py:218
  110.6 11.5 %all-to-all-start = ((bf16[4,512,128]{2,1,0:T(8,128)(2,1)}), bf16[4,512,128]{2,1,0:T(8,128)(2,1)S(1)}, u32[]{:S(2)}, u32[]{:S(2)}) async-start(bf16[4,512,128]{2,1,0:T(8,128)(2,1)} %edge_rows.1), calls=%async_computation | async-start | bytes 1048576 | tf_op jit(solution)/shard_map/all_to_all | solution.py:228
  122.8 13.8 %all-to-all-start.4 = ((f32[32,16,128]{2,1,0:T(8,128)}), f32[32,16,128]{2,1,0:T(8,128)S(1)}, u32[]{:S(2)}, u32[]{:S(2)}) async-start(f32[32,16,128]{2,1,0:T(8,128)} %broadcast_in_dim.30), calls=%async_computation.4 | async-start | bytes 524288 | tf_op jit(solution)/shard_map/all_to_all | solution.py:236
  (7 other events, 13.1 us)

commit v2 on v0

v2 whole, which is shorter than its diff:
```python
import jax
import jax.numpy as jnp
from jax import lax
from jax.experimental import pallas as pl
from jax.experimental.pallas import tpu as pltpu
from jax.sharding import PartitionSpec as P

BW = 8
RB = 128
NBLK = 1024
T = 128
QUADS = 8
SLOTS = 5
RC = ("row", "col")
RD = ("row", "depth")
bf16 = jnp.bfloat16
SMALL = pl.CostEstimate(flops=1024, bytes_accessed=1024, transcendentals=0)
f32 = jnp.float32


def ring(n, shift):
    return [(i, (i + shift) % n) for i in range(n)]


def flip(bit):
    return [(i, i ^ bit) for i in range(4)]


def params(mib):
    return pltpu.CompilerParams(vmem_limit_bytes=mib << 20)


ANY = pl.BlockSpec(memory_space=pl.ANY)
SMEM = pl.BlockSpec(memory_space=pltpu.SMEM)
VMEM = pl.BlockSpec(memory_space=pltpu.VMEM)


def densify_kernel(inv, tiles, out, held, sem):
    per = SLOTS * 4

    for k in range(QUADS * per):
        at = inv[k]
        pltpu.make_async_copy(
            tiles.at[0, 0, jnp.where(at >= 0, at, k)], held.at[k // per, k % per], sem.at[k // per]
        ).start()
    for q in range(QUADS):
        pltpu.make_async_copy(held.at[q], held.at[q], sem.at[q]).wait()
        for k in range(per):
            slot, e = k // 4, k % 4
            turned = jnp.where(inv[q * per + k] >= 0, held[q, k].T, jnp.zeros((T, T), bf16))
            out[q, slot * T:(slot + 1) * T, e * T:(e + 1) * T] = turned


def densify(inv, tile_values):
    return pl.pallas_call(
        densify_kernel,
        in_specs=[SMEM, ANY],
        out_specs=VMEM,
        out_shape=jax.ShapeDtypeStruct((QUADS, SLOTS * T, 4 * T), bf16),
        scratch_shapes=[pltpu.VMEM((QUADS, SLOTS * 4, T, T), bf16), pltpu.SemaphoreType.DMA((QUADS,))],
        compiler_params=params(42),
        cost_estimate=SMALL,
        name="densify",
    )(inv, tile_values)


def columns_kernel(depth, band, n0, n1, n2, n3, f0, f1, f2, f3, w0, w1, w2, w3, *refs):
    parts, (acc, weight) = refs[0:4], refs[4:]
    for s, w in enumerate((w0, w1, w2, w3)):
        weight[:, s * T:(s + 1) * T] = w[8 * T:12 * T, :]
    acc[...] = jnp.zeros_like(acc)
    for q in range(QUADS):
        sides = [jnp.concatenate([part[q * T:(q + 1) * T] for part in (n0, n1, n2, n3)], axis=0)]
        for s in range(3):
            at = slice((8 * s + q) * T, (8 * s + q + 1) * T)
            sides.append(jnp.concatenate([part[at] for part in (f0, f1, f2, f3)], axis=0))
        acc[q * T:(q + SLOTS) * T, :] += jnp.dot(
            band[q], jnp.concatenate(sides, axis=1), preferred_element_type=f32
        )
    for k in range(6):
        rows = slice(k * 2 * T, (k + 1) * 2 * T)
        spread = acc[rows, :].astype(bf16)
        for t in range(4):
            src = pl.ds(pl.multiple_of((depth[0] + t) % 4 * T, T), T)
            got = lax.dot_general(
                spread, weight[src, :], (((1,), (1,)), ((), ())), preferred_element_type=f32
            ).astype(bf16)
            parts[t][rows, :] = got


def columns(depth, band, near, far, given):
    return pl.pallas_call(
        columns_kernel,
        in_specs=[SMEM] + [VMEM] * 13,
        out_specs=[VMEM] * 4,
        out_shape=[jax.ShapeDtypeStruct((12 * T, T), bf16)] * 4,
        scratch_shapes=[pltpu.VMEM((12 * T, 4 * T), f32), pltpu.VMEM((4 * T, 4 * T), bf16)],
        compiler_params=params(12),
        cost_estimate=SMALL,
        name="columns",
    )(depth, band, *near, *far, *given)


def place_kernel(depth, r0, r1, r2, r3, following, previous, out, ends):
    ends[0, 2 * T:4 * T] = previous[...]
    ends[5, 0:2 * T] = following[...]
    for t, part in enumerate((r0, r1, r2, r3)):
        k = (depth[0] - t + 4) % 4
        ends[k + 1, 0:2 * T] = part[0:2 * T, :]
        ends[k + 1, 2 * T:4 * T] = part[10 * T:12 * T, :]
    for t, part in enumerate((r0, r1, r2, r3)):
        k = (depth[0] - t + 4) % 4
        before = ends[k, 2 * T:4 * T].astype(f32)
        behind = ends[k + 2, 0:2 * T].astype(f32)
        out[k, 0:2 * T] = (part[2 * T:4 * T, :].astype(f32) + before).astype(bf16)
        out[k, 2 * T:6 * T] = part[4 * T:8 * T, :]
        out[k, 6 * T:8 * T] = (part[8 * T:10 * T, :].astype(f32) + behind).astype(bf16)


def place(depth, parts, following, previous):
    return pl.pallas_call(
        place_kernel,
        in_specs=[SMEM] + [VMEM] * 6,
        out_specs=VMEM,
        out_shape=jax.ShapeDtypeStruct((4, 8 * T, T), bf16),
        scratch_shapes=[pltpu.VMEM((6, 4 * T, T), bf16)],
        compiler_params=params(8),
        cost_estimate=SMALL,
        name="place",
    )(depth, *parts, following, previous)


def outer_kernel(depth, g0, g1, g2, g3, own, more, out, turned):
    for s in range(4):
        dst = pl.ds(pl.multiple_of(((depth[0] - s + 4) % 4) * T, T), T)
        turned[:, dst] = own[...] if s == 0 else more[(s - 1) * 8 * T:s * 8 * T, :]
    for s, g in enumerate((g0, g1, g2, g3)):
        a = (depth[0] - s + 4) % 4
        got = lax.dot_general(
            g[0:8 * T, :], turned[...], (((0,), (0,)), ((), ())), preferred_element_type=f32
        ).astype(bf16)
        for t in range(4):
            out[pl.ds(a * 8, 8), t] = got[:, t * T:(t + 1) * T].reshape(8, 16, T)


def outer(depth, given, own, more):
    return pl.pallas_call(
        outer_kernel,
        in_specs=[SMEM] + [VMEM] * 6,
        out_specs=VMEM,
        out_shape=jax.ShapeDtypeStruct((32, 4, 16, T), bf16),
        scratch_shapes=[pltpu.VMEM((8 * T, 4 * T), bf16)],
        compiler_params=params(8),
        cost_estimate=SMALL,
        name="outer",
    )(depth, *given, own, more)


def after(value, *others):
    return lax.optimization_barrier((value, others))[0]


def inverse_table(rows, cols, count, stripe, col, depth):
    slot_ids = jnp.arange(rows.shape[0], dtype=jnp.int32)
    shift = (cols - (stripe * RB + rows) + BW) % NBLK
    within = rows % 32
    quad = within // 4
    slot = (within + shift - col) // 4 - quad
    key = (quad * SLOTS + slot) * 4 + ((rows % 4) ^ col)
    key = jnp.where((slot_ids < count) & (rows // 32 == depth), key, -1)
    targets = jnp.arange(QUADS * SLOTS * 4, dtype=jnp.int32)
    return jnp.max(jnp.where(key[None, :] == targets[:, None], slot_ids[None, :], -1), axis=1)


def local(out_grad, relu_mask, aggregated, weight, tile_values, tile_rows, tile_cols, tile_count):
    stripe = lax.axis_index("row")
    col = lax.axis_index("col")
    depth = lax.axis_index("depth")

    def other(array):
        return lax.ppermute(array, "col", flip(2))

    def pair(array):
        return lax.ppermute(array, "col", flip(1))

    depth1 = depth.reshape(1).astype(jnp.int32)

    def quarter(array, t):
        return lax.dynamic_slice_in_dim(array, ((depth + t) % 4) * 1024, 1024)

    def masked(grads, mask, t):
        return jnp.where(quarter(mask, t) != 0, quarter(grads, t), jnp.zeros((), bf16))

    def from_depth(array, t):
        return lax.ppermute(array, "depth", ring(4, t))

    own = masked(out_grad, relu_mask, 0)
    zed = other(own)
    near = (own, pair(own), zed, pair(zed))
    grads, mask = after((out_grad, relu_mask), own)
    rows = {t: from_depth(masked(grads, mask, t), t) for t in (2, 1, 3)}

    more = jnp.concatenate([rows[1], rows[2], rows[3]], axis=0)
    zed = other(after(more, zed))
    late, late_weight = after((aggregated, weight), more)
    given = [jnp.concatenate([quarter(late, t), late_weight], axis=0) for t in range(4)]
    given = given[:1] + [from_depth(given[t], t) for t in (1, 2, 3)]
    inv = inverse_table(tile_rows[0, 0], tile_cols[0, 0], tile_count[0, 0], stripe, col, depth)
    band = densify(after(inv, more), tile_values)

    pieces = outer(depth1, given, own, more).reshape(128, 16, T)
    far = (more, pair(more), zed, pair(after(zed, band, pieces)))
    pieces = lax.all_to_all(pieces, ("row", "col", "depth"), 0, 0)

    res = columns(depth1, band, near, far, given)
    back = [res[0]] + [from_depth(res[t], t) for t in (1, 2, 3)]

    def of_quarter(k, rows):
        parts = [back[t][rows] for t in range(4)]
        t = (depth - k) % 4
        return jnp.where(t < 2, jnp.where(t == 0, parts[0], parts[1]), jnp.where(t == 2, parts[2], parts[3]))

    following = lax.ppermute(of_quarter(0, slice(0, 2 * T)), "row", ring(8, -1))
    previous = lax.ppermute(of_quarter(3, slice(10 * T, 12 * T)), "row", ring(8, 1))
    grad_input = place(depth1, back, following, previous).reshape(32 * T, T)

    piece = jnp.sum(after(pieces, res[0]).astype(f32), axis=0)
    grad_weight = lax.all_to_all(jnp.broadcast_to(piece, (32, 16, T)), RC, 0, 0).reshape(4 * T, T)
    return grad_input, grad_weight


def solution(mesh):
    placed = (
        P(RC, "depth"),
        P(RC, "depth"),
        P(RC, "depth"),
        P(None, "depth"),
        P("row", "col", None, None, None),
        P("row", "col", None),
        P("row", "col", None),
        P("row", "col"),
    )
    return jax.shard_map(
        local,
        mesh=mesh,
        in_specs=placed,
        out_specs=(P(RC, "depth"), P(None, "depth")),
        check_vma=False,
    )
```

time: 483 us -> 104 us (0.22)
  waiting for transfers between devices: 247 us -> 32 us
  other arithmetic: 115 us -> 6.46 us
  local copies, waits for them, and re-layouts: 64.2 us -> 8.83 us
  starting transfers between devices: 4.29 us -> 41.4 us
  matrix products: 35.1 us -> 0 us
  Pallas kernels: 0 us -> 13.8 us
  between operations: 14.5 us -> 1.55 us
    scatter-add x1 -> x0, other arithmetic: 106 us -> none  [local(): buffer = jax.ops.segment_sum(contrib, segment, num_segments=3 * col_blocks)]
    reduce_scatter x1 -> x0, waiting for transfers between devices: 80.7 us -> none  [local(): lax.psum_scatter(partial_terms, 'depth', scatter_dimension=1, tiled=True)]
    ppermute x2 -> x17, waiting for transfers between devices: 87.2 us -> 32 us  [the longest x9 24 us: from_depth(): return lax.ppermute(array, 'depth', ring(4, t))]
    all_gather x2 -> x0, waiting for transfers between devices: 39.7 us -> none  [the longest x1 39.7 us: local(): stripe_grad = lax.all_gather(out_masked, 'col', axis=0, tiled=True)]
    psum x1 -> x0, waiting for transfers between devices: 38.6 us -> none  [local(): grad_weight = lax.psum(weight_terms, ('row', 'col'))]
    dot_general x1 -> x0, local copies, waits for them, and re-layouts: 35.6 us -> none  [local(): jnp.einsum('sij,sif->sjf', tile_values[0, 0], picked, preferred_element_t...]
    dot_general x3 -> x0, matrix products: 35.1 us -> none  [the longest x1 27 us: local(): jnp.einsum('sij,sif->sjf', tile_values[0, 0], picked, preferred_element_t...]
    ppermute x2 -> x17, starting transfers between devices: 4.14 us -> 27.7 us  [the longest x9 15.6 us: from_depth(): return lax.ppermute(array, 'depth', ring(4, t))]
  transfers between devices with their start and end apart: 6 -> 19, of which waited for: 5 -> 9; matrix products, arithmetic and copies ran while one was open for 43% -> 4% of each run, Pallas kernels for 0% -> 12%
where the time goes in v2:
time: 104 us
  starting transfers between devices  41.4 us (40%)
  waiting for transfers between devices  32 us (31%)
  Pallas kernels  13.8 us (13%)
  local copies, waits for them, and re-layouts  8.83 us (8%)
  other arithmetic  6.46 us (6%)
  between operations  1.55 us (1%)
    ppermute x9, waiting for transfers between devices, from_depth(): return lax.ppermute(array, 'depth', ring(4, t))  24 us
    ppermute x9, starting transfers between devices, from_depth(): return lax.ppermute(array, 'depth', ring(4, t))  15.6 us
    unnamed x23, local copies, waits for them, and re-layouts  8 us
    ppermute x2, starting transfers between devices, other(): return lax.ppermute(array, 'col', flip(2))  7.75 us
    all_to_all x1, starting transfers between devices, local(): lax.all_to_all(jnp.broadcast_to(piece, (32, 16, T)), RC, 0, 0)  7.59 us
    pallas_call x1, Pallas kernels, columns(): pl.pallas_call(columns_kernel, in_specs=[SMEM] + [VMEM] * 13, out_specs=[...  6.81 us
    all_to_all x1, starting transfers between devices, local(): pieces = lax.all_to_all(pieces, ('row', 'col', 'depth'), 0, 0)  6.06 us
    ppermute x1, waiting for transfers between devices, local(): lax.ppermute(of_quarter(3, slice(10 * T, 12 * T)), 'row', ring(8, 1))  4.47 us
  transfers between devices with their start and end apart: 19, of which 9 were waited for; matrix products, arithmetic and copies ran while one was open for 4% of the time, Pallas kernels for 12%

profile of v2, /device:TPU:0, one launch (start us, length us, event | category | flops | bytes accessed | tf_op | source)
XLA Modules:
  0.0 104.0 jit_solution(587939795381242433)
XLA Ops:
  1.9 1.9 %fusion.3 = (bf16[1024,128]{1,0:T(8,128)(2,1)S(1)}, bf16[1024,128]{1,0:T(8,128)(2,1)S(1)}, bf16[1024,128]{1,0:T(8,128)(2,1)S(1)}) fusion(s32[4096,128]{1,0:T(8,128)} %param.9, s32[]{:T(128)S(6)} %select_n.191, bf16[4096,128]{1,0:T(8,128)(2,1)} %param.8, s32[]{:T(128)S(6)} %select_n.188, s32[]{:T(128)S(6)} %select_n.185), kind=kLoop, calls=%fused_computation.12 | loop fusion | flops 786432 | bytes 3145740 | tf_op jit(solution)/shard_map/jit(_where)/select_n | solution.py:192
  3.8 1.7 %collective-permute-start = (bf16[1024,128]{1,0:T(8,128)(2,1)S(1)}, bf16[1024,128]{1,0:T(8,128)(2,1)S(1)}, u32[]{:S(2)}, u32[]{:S(2)}) collective-permute-start(bf16[1024,128]{1,0:T(8,128)(2,1)S(1)} %get-tuple-element.28), channel_id=1, source_target_pairs={{0,1},{1,2},{2,3},{3,0},{4,5},{5,6},{6,7},{7,4},{8,9},{9,10},{10,1... | collective-permute-start | bytes 786440 | tf_op jit(solution)/shard_map/ppermute | solution.py:195
  5.5 2.9 %collective-permute-start.1 = (bf16[1024,128]{1,0:T(8,128)(2,1)S(1)}, bf16[1024,128]{1,0:T(8,128)(2,1)S(1)}, u32[]{:S(2)}, u32[]{:S(2)}) collective-permute-start(bf16[1024,128]{1,0:T(8,128)(2,1)S(1)} %get-tuple-element.27), channel_id=1, source_target_pairs={{0,2},{1,3},{2,0},{3,1},{4,6},{5,7},{6,4},{7,5},{8,10},{9,11},{10,... | collective-permute-start | bytes 786440 | tf_op jit(solution)/shard_map/ppermute | solution.py:195
  8.4 1.3 %collective-permute-start.2 = (bf16[1024,128]{1,0:T(8,128)(2,1)S(1)}, bf16[1024,128]{1,0:T(8,128)(2,1)S(1)}, u32[]{:S(2)}, u32[]{:S(2)}) collective-permute-start(bf16[1024,128]{1,0:T(8,128)(2,1)S(1)} %get-tuple-element.26), channel_id=1, source_target_pairs={{0,3},{1,0},{2,1},{3,2},{4,7},{5,4},{6,5},{7,6},{8,11},{9,8},{10,9... | collective-permute-start | bytes 786440 | tf_op jit(solution)/shard_map/ppermute | solution.py:195
  9.8 3.9 %collective-permute-start.4 = (bf16[1024,128]{1,0:T(8,128)(2,1)S(1)}, bf16[1024,128]{1,0:T(8,128)(2,1)S(1)}, u32[]{:S(2)}, u32[]{:S(2)}) collective-permute-start(bf16[1024,128]{1,0:T(8,128)(2,1)S(1)} %fusion.own.n0), channel_id=1, source_target_pairs={{0,8},{4,12},{8,0},{12,4},{1,9},{5,13},{9,1},{13,5},{2,10},{6,14},... | collective-permute-start | bytes 786440 | tf_op jit(solution)/shard_map/ppermute | solution.py:181
  13.7 6.4 %collective-permute-done.1 = bf16[1024,128]{1,0:T(8,128)(2,1)S(1)} collective-permute-done((bf16[1024,128]{1,0:T(8,128)(2,1)S(1)}, bf16[1024,128]{1,0:T(8,128)(2,1)S(1)}, u32[]{:S(2)}, u32[]{:S(2)}) %collective-permute-start.1) | collective-permute-done | bytes 262176 | tf_op jit(solution)/shard_map/ppermute | solution.py:195
  20.9 3.9 %collective-permute-start.7 = (bf16[3072,128]{1,0:T(8,128)(2,1)S(1)}, bf16[3072,128]{1,0:T(8,128)(2,1)S(1)}, u32[]{:S(2)}, u32[]{:S(2)}) collective-permute-start(bf16[3072,128]{1,0:T(8,128)(2,1)S(1)} %constant_dynamic-update-slice_fusion.more.f0), channel_id=1, source_target_pairs={{0,8},{4,12},{8,0},{12,4},{1,9},{5,13},{9,1},{13,5},{2,10},{6,14},... | collective-permute-start | bytes 2359304 | tf_op jit(solution)/shard_map/ppermute | solution.py:181
  26.0 2.1 %collective-permute-start.10 = (bf16[1536,128]{1,0:T(8,128)(2,1)}, bf16[1536,128]{1,0:T(8,128)(2,1)S(1)}, u32[]{:S(2)}, u32[]{:S(2)}) collective-permute-start(bf16[1536,128]{1,0:T(8,128)(2,1)} %get-tuple-element.35), channel_id=1, source_target_pairs={{0,3},{1,0},{2,1},{3,2},{4,7},{5,4},{6,5},{7,6},{8,11},{9,8},{10,9... | collective-permute-start | bytes 1179656 | tf_op jit(solution)/shard_map/ppermute | solution.py:195
  28.1 2.4 %collective-permute-start.9 = (bf16[1536,128]{1,0:T(8,128)(2,1)}, bf16[1536,128]{1,0:T(8,128)(2,1)S(1)}, u32[]{:S(2)}, u32[]{:S(2)}) collective-permute-start(bf16[1536,128]{1,0:T(8,128)(2,1)} %get-tuple-element.37), channel_id=1, source_target_pairs={{0,2},{1,3},{2,0},{3,1},{4,6},{5,7},{6,4},{7,5},{8,10},{9,11},{10,... | collective-permute-start | bytes 1179656 | tf_op jit(solution)/shard_map/ppermute | solution.py:195
  31.5 4.1 %densify.1.band = bf16[8,640,512]{2,1,0:T(8,128)(2,1)S(1)} custom-call(s32[160]{0:T(256)S(1)} %select_reduce_fusion.inv, bf16[1,1,544,128,128]{4,3,2,1,0:T(8,128)(2,1)} %tiles.1), custom_call_target="tpu_custom_call" | custom-call | flops 1024 | bytes 1024 | tf_op jit(solution)/shard_map/densify/pallas_call | solution.py:55
  35.6 2.3 %copy-done = bf16[8,640,512]{2,1,0:T(8,128)(2,1)} copy-done((bf16[8,640,512]{2,1,0:T(8,128)(2,1)}, bf16[8,640,512]{2,1,0:T(8,128)(2,1)S(1)}, u32[]{:S(2)}) %copy-start) | copy-done | bytes 5242904
  37.9 7.2 %collective-permute-done.10.g3.w3 = bf16[1536,128]{1,0:T(8,128)(2,1)S(1)} collective-permute-done((bf16[1536,128]{1,0:T(8,128)(2,1)}, bf16[1536,128]{1,0:T(8,128)(2,1)S(1)}, u32[]{:S(2)}, u32[]{:S(2)}) %collective-permute-start.10) | collective-permute-done | bytes 393248 | tf_op jit(solution)/shard_map/ppermute | solution.py:195
  45.1 3.3 %collective-permute-done.8.g1.w1 = bf16[1536,128]{1,0:T(8,128)(2,1)S(1)} collective-permute-done((bf16[1536,128]{1,0:T(8,128)(2,1)}, bf16[1536,128]{1,0:T(8,128)(2,1)S(1)}, u32[]{:S(2)}, u32[]{:S(2)}) %collective-permute-start.8) | collective-permute-done | bytes 393248 | tf_op jit(solution)/shard_map/ppermute | solution.py:195
  48.4 1.8 %outer.1 = bf16[32,4,16,128]{3,2,1,0:T(8,128)(2,1)} custom-call(s32[1]{0:T(128)} %bitcast.depth, bf16[1536,128]{1,0:T(8,128)(2,1)S(1)} %get-tuple-element.38.g0.w0, bf16[1536,128]{1,0:T(8,128)(2,1)S(1)} %collective-permute-done.8.g1.w1, bf16[1536,128]{1,0:T(8,128)(2,1)S(1)} %collective-permute-done.9.g2.w2, ...), custom_call_target="tpu_custom_call" | custom-call | flops 1024 | bytes 1024 | tf_op jit(solution)/shard_map/outer/pallas_call | solution.py:147
  50.2 6.1 %all-to-all-start = ((bf16[128,16,128]{2,1,0:T(8,128)(2,1)}), bf16[128,16,128]{2,1,0:T(8,128)(2,1)}, u32[]{:S(2)}, u32[]{:S(2)}) async-start(bf16[128,16,128]{2,1,0:T(8,128)(2,1)} %bitcast.2), calls=%async_computation | async-start | bytes 1048576 | tf_op jit(solution)/shard_map/all_to_all | solution.py:213
  58.4 2.5 %copy-done.1 = bf16[8,640,512]{2,1,0:T(8,128)(2,1)S(1)} copy-done((bf16[8,640,512]{2,1,0:T(8,128)(2,1)S(1)}, bf16[8,640,512]{2,1,0:T(8,128)(2,1)}, u32[]{:S(2)}) %copy-start.1) | copy-done | bytes 5242904
  61.9 6.8 %columns.1 = (bf16[1536,128]{1,0:T(8,128)(2,1)S(1)}, bf16[1536,128]{1,0:T(8,128)(2,1)}, bf16[1536,128]{1,0:T(8,128)(2,1)}, bf16[1536,128]{1,0:T(8,128)(2,1)}) custom-call(s32[1]{0:T(128)} %bitcast.depth, bf16[8,640,512]{2,1,0:T(8,128)(2,1)S(1)} %copy-done.1, bf16[1024,128]{1,0:T(8,128)(2,1)S(1)} %fusion.own.n0, ...), custom_call_target="tpu_custom_call" | custom-call | flops 1024 | bytes 1024 | tf_op jit(solution)/shard_map/columns/pallas_call | solution.py:92
  70.3 2.7 %collective-permute-start.13 = (bf16[1536,128]{1,0:T(8,128)(2,1)}, bf16[1536,128]{1,0:T(8,128)(2,1)S(1)}, u32[]{:S(2)}, u32[]{:S(2)}) collective-permute-start(bf16[1536,128]{1,0:T(8,128)(2,1)} %get-tuple-element.23), channel_id=1, source_target_pairs={{0,2},{1,3},{2,0},{3,1},{4,6},{5,7},{6,4},{7,5},{8,10},{9,11},{10,... | collective-permute-start | bytes 1179656 | tf_op jit(solution)/shard_map/ppermute | solution.py:195
  73.1 1.4 %collective-permute-start.14 = (bf16[1536,128]{1,0:T(8,128)(2,1)}, bf16[1536,128]{1,0:T(8,128)(2,1)S(1)}, u32[]{:S(2)}, u32[]{:S(2)}) collective-permute-start(bf16[1536,128]{1,0:T(8,128)(2,1)} %get-tuple-element.24), channel_id=1, source_target_pairs={{0,3},{1,0},{2,1},{3,2},{4,7},{5,4},{6,5},{7,6},{8,11},{9,8},{10,9... | collective-permute-start | bytes 1179656 | tf_op jit(solution)/shard_map/ppermute | solution.py:195
  76.4 7.6 %all-to-all-start.1 = ((f32[32,16,128]{2,1,0:T(8,128)}), f32[32,16,128]{2,1,0:T(8,128)S(1)}, u32[]{:S(2)}, u32[]{:S(2)}) async-start(f32[32,16,128]{2,1,0:T(8,128)} %broadcast_in_dim.30), calls=%async_computation.1 | async-start | bytes 524288 | tf_op jit(solution)/shard_map/all_to_all | solution.py:228
  84.0 6.8 %collective-permute-done.13.r2 = bf16[1536,128]{1,0:T(8,128)(2,1)S(1)} collective-permute-done((bf16[1536,128]{1,0:T(8,128)(2,1)}, bf16[1536,128]{1,0:T(8,128)(2,1)S(1)}, u32[]{:S(2)}, u32[]{:S(2)}) %collective-permute-start.13) | collective-permute-done | bytes 393248 | tf_op jit(solution)/shard_map/ppermute | solution.py:195
  92.0 3.7 %collective-permute-start.15 = (bf16[256,128]{1,0:T(8,128)(2,1)S(1)}, bf16[256,128]{1,0:T(8,128)(2,1)S(1)}, u32[]{:S(2)}, u32[]{:S(2)}) collective-permute-start(bf16[256,128]{1,0:T(8,128)(2,1)S(1)} %get-tuple-element.30), channel_id=1, source_target_pairs={{0,112},{16,0},{32,16},{48,32},{64,48},{80,64},{96,80},{112,96},{1... | collective-permute-start | bytes 196616 | tf_op jit(solution)/shard_map/ppermute | solution.py:223
  95.7 1.9 %collective-permute-done.15.following = bf16[256,128]{1,0:T(8,128)(2,1)S(1)} collective-permute-done((bf16[256,128]{1,0:T(8,128)(2,1)S(1)}, bf16[256,128]{1,0:T(8,128)(2,1)S(1)}, u32[]{:S(2)}, u32[]{:S(2)}) %collective-permute-start.15) | collective-permute-done | bytes 65568 | tf_op jit(solution)/shard_map/ppermute | solution.py:223
  97.6 4.5 %collective-permute-done.16.previous = bf16[256,128]{1,0:T(8,128)(2,1)S(1)} collective-permute-done((bf16[256,128]{1,0:T(8,128)(2,1)S(1)}, bf16[256,128]{1,0:T(8,128)(2,1)S(1)}, u32[]{:S(2)}, u32[]{:S(2)}) %collective-permute-start.16) | collective-permute-done | bytes 65568 | tf_op jit(solution)/shard_map/ppermute | solution.py:224
  (53 shorter events, 13.2 us)
Async XLA Ops:
  1.9 22.9 %copy-start.6 = (bf16[4096,128]{1,0:T(8,128)(2,1)S(1)}, bf16[4096,128]{1,0:T(8,128)(2,1)}, u32[]{:S(2)}) copy-start(bf16[4096,128]{1,0:T(8,128)(2,1)} %param.10) | copy-start | bytes 3145732
  3.8 21.1 %copy-start.7 = (bf16[512,128]{1,0:T(8,128)(2,1)S(1)}, bf16[512,128]{1,0:T(8,128)(2,1)}, u32[]{:S(2)}) copy-start(bf16[512,128]{1,0:T(8,128)(2,1)} %param.11) | copy-start | bytes 393220
  3.8 9.9 %collective-permute-start = (bf16[1024,128]{1,0:T(8,128)(2,1)S(1)}, bf16[1024,128]{1,0:T(8,128)(2,1)S(1)}, u32[]{:S(2)}, u32[]{:S(2)}) collective-permute-start(bf16[1024,128]{1,0:T(8,128)(2,1)S(1)} %get-tuple-element.28), channel_id=1, source_target_pairs={{0,1},{1,2},{2,3},{3,0},{4,5},{5,6},{6,7},{7,4},{8,9},{9,10},{10,1... | collective-permute-start | bytes 786440 | tf_op jit(solution)/shard_map/ppermute | solution.py:195
  5.5 14.5 %collective-permute-start.1 = (bf16[1024,128]{1,0:T(8,128)(2,1)S(1)}, bf16[1024,128]{1,0:T(8,128)(2,1)S(1)}, u32[]{:S(2)}, u32[]{:S(2)}) collective-permute-start(bf16[1024,128]{1,0:T(8,128)(2,1)S(1)} %get-tuple-element.27), channel_id=1, source_target_pairs={{0,2},{1,3},{2,0},{3,1},{4,6},{5,7},{6,4},{7,5},{8,10},{9,11},{10,... | collective-permute-start | bytes 786440 | tf_op jit(solution)/shard_map/ppermute | solution.py:195
  8.4 11.7 %collective-permute-start.2 = (bf16[1024,128]{1,0:T(8,128)(2,1)S(1)}, bf16[1024,128]{1,0:T(8,128)(2,1)S(1)}, u32[]{:S(2)}, u32[]{:S(2)}) collective-permute-start(bf16[1024,128]{1,0:T(8,128)(2,1)S(1)} %get-tuple-element.26), channel_id=1, source_target_pairs={{0,3},{1,0},{2,1},{3,2},{4,7},{5,4},{6,5},{7,6},{8,11},{9,8},{10,9... | collective-permute-start | bytes 786440 | tf_op jit(solution)/shard_map/ppermute | solution.py:195
  9.8 10.4 %collective-permute-start.4 = (bf16[1024,128]{1,0:T(8,128)(2,1)S(1)}, bf16[1024,128]{1,0:T(8,128)(2,1)S(1)}, u32[]{:S(2)}, u32[]{:S(2)}) collective-permute-start(bf16[1024,128]{1,0:T(8,128)(2,1)S(1)} %fusion.own.n0), channel_id=1, source_target_pairs={{0,8},{4,12},{8,0},{12,4},{1,9},{5,13},{9,1},{13,5},{2,10},{6,14},... | collective-permute-start | bytes 786440 | tf_op jit(solution)/shard_map/ppermute | solution.py:181
  20.2 10.4 %copy-start.8 = (s32[1,1,544]{2,1,0:T(1,128)S(1)}, s32[1,1,544]{2,1,0:T(1,128)}, u32[]{:S(2)}) copy-start(s32[1,1,544]{2,1,0:T(1,128)} %param.13) | copy-start | bytes 6532
  20.2 10.4 %copy-start.9 = (s32[1,1,544]{2,1,0:T(1,128)S(1)}, s32[1,1,544]{2,1,0:T(1,128)}, u32[]{:S(2)}) copy-start(s32[1,1,544]{2,1,0:T(1,128)} %param.14) | copy-start | bytes 6532
  20.9 29.3 %collective-permute-start.7 = (bf16[3072,128]{1,0:T(8,128)(2,1)S(1)}, bf16[3072,128]{1,0:T(8,128)(2,1)S(1)}, u32[]{:S(2)}, u32[]{:S(2)}) collective-permute-start(bf16[3072,128]{1,0:T(8,128)(2,1)S(1)} %constant_dynamic-update-slice_fusion.more.f0), channel_id=1, source_target_pairs={{0,8},{4,12},{8,0},{12,4},{1,9},{5,13},{9,1},{13,5},{2,10},{6,14},... | collective-permute-start | bytes 2359304 | tf_op jit(solution)/shard_map/ppermute | solution.py:181
  26.0 19.1 %collective-permute-start.10 = (bf16[1536,128]{1,0:T(8,128)(2,1)}, bf16[1536,128]{1,0:T(8,128)(2,1)S(1)}, u32[]{:S(2)}, u32[]{:S(2)}) collective-permute-start(bf16[1536,128]{1,0:T(8,128)(2,1)} %get-tuple-element.35), channel_id=1, source_target_pairs={{0,3},{1,0},{2,1},{3,2},{4,7},{5,4},{6,5},{7,6},{8,11},{9,8},{10,9... | collective-permute-start | bytes 1179656 | tf_op jit(solution)/shard_map/ppermute | solution.py:195
  28.1 20.3 %collective-permute-start.8 = (bf16[1536,128]{1,0:T(8,128)(2,1)}, bf16[1536,128]{1,0:T(8,128)(2,1)S(1)}, u32[]{:S(2)}, u32[]{:S(2)}) collective-permute-start(bf16[1536,128]{1,0:T(8,128)(2,1)} %get-tuple-element.36), channel_id=1, source_target_pairs={{0,1},{1,2},{2,3},{3,0},{4,5},{5,6},{6,7},{7,4},{8,9},{9,10},{10,1... | collective-permute-start | bytes 1179656 | tf_op jit(solution)/shard_map/ppermute | solution.py:195
  28.1 20.3 %collective-permute-start.9 = (bf16[1536,128]{1,0:T(8,128)(2,1)}, bf16[1536,128]{1,0:T(8,128)(2,1)S(1)}, u32[]{:S(2)}, u32[]{:S(2)}) collective-permute-start(bf16[1536,128]{1,0:T(8,128)(2,1)} %get-tuple-element.37), channel_id=1, source_target_pairs={{0,2},{1,3},{2,0},{3,1},{4,6},{5,7},{6,4},{7,5},{8,10},{9,11},{10,... | collective-permute-start | bytes 1179656 | tf_op jit(solution)/shard_map/ppermute | solution.py:195
  31.4 27.0 %collective-permute-start.6 = (bf16[3072,128]{1,0:T(8,128)(2,1)S(1)}, bf16[3072,128]{1,0:T(8,128)(2,1)}, u32[]{:S(2)}, u32[]{:S(2)}) collective-permute-start(bf16[3072,128]{1,0:T(8,128)(2,1)S(1)} %constant_dynamic-update-slice_fusion.more.f0), channel_id=1, source_target_pairs={{0,4},{4,0},{8,12},{12,8},{1,5},{5,1},{9,13},{13,9},{2,6},{6,2},{1... | collective-permute-start | bytes 2359304 | tf_op jit(solution)/shard_map/ppermute | solution.py:184
  50.2 8.3 %collective-permute-start.11 = (bf16[3072,128]{1,0:T(8,128)(2,1)S(1)}, bf16[3072,128]{1,0:T(8,128)(2,1)}, u32[]{:S(2)}, u32[]{:S(2)}) collective-permute-start(bf16[3072,128]{1,0:T(8,128)(2,1)S(1)} %collective-permute-done.7.f2), channel_id=1, source_target_pairs={{0,4},{4,0},{8,12},{12,8},{1,5},{5,1},{9,13},{13,9},{2,6},{6,2},{1... | collective-permute-start | bytes 2359304 | tf_op jit(solution)/shard_map/ppermute | solution.py:184
  50.2 24.3 %all-to-all-start = ((bf16[128,16,128]{2,1,0:T(8,128)(2,1)}), bf16[128,16,128]{2,1,0:T(8,128)(2,1)}, u32[]{:S(2)}, u32[]{:S(2)}) async-start(bf16[128,16,128]{2,1,0:T(8,128)(2,1)} %bitcast.2), calls=%async_computation | async-start | bytes 1048576 | tf_op jit(solution)/shard_map/all_to_all | solution.py:213
  56.2 1.6 %collective-permute-start.3 = (bf16[1024,128]{1,0:T(8,128)(2,1)S(1)}, bf16[1024,128]{1,0:T(8,128)(2,1)S(1)}, u32[]{:S(2)}, u32[]{:S(2)}) collective-permute-start(bf16[1024,128]{1,0:T(8,128)(2,1)S(1)} %fusion.own.n0), channel_id=1, source_target_pairs={{0,4},{4,0},{8,12},{12,8},{1,5},{5,1},{9,13},{13,9},{2,6},{6,2},{1... | collective-permute-start | bytes 786440 | tf_op jit(solution)/shard_map/ppermute | solution.py:184
  56.3 2.1 %collective-permute-start.5 = (bf16[1024,128]{1,0:T(8,128)(2,1)}, bf16[1024,128]{1,0:T(8,128)(2,1)S(1)}, u32[]{:S(2)}, u32[]{:S(2)}) collective-permute-start(bf16[1024,128]{1,0:T(8,128)(2,1)} %copy-done.4), channel_id=1, source_target_pairs={{0,4},{4,0},{8,12},{12,8},{1,5},{5,1},{9,13},{13,9},{2,6},{6,2},{1... | collective-permute-start | bytes 786440 | tf_op jit(solution)/shard_map/ppermute | solution.py:184
  69.4 32.6 %copy-start.3 = (bf16[1536,128]{1,0:T(8,128)(2,1)S(1)}, bf16[1536,128]{1,0:T(8,128)(2,1)}, u32[]{:S(2)}) copy-start(bf16[1536,128]{1,0:T(8,128)(2,1)} %copy-done.2) | copy-start | bytes 1179652
  69.4 14.5 %collective-permute-start.12 = (bf16[1536,128]{1,0:T(8,128)(2,1)}, bf16[1536,128]{1,0:T(8,128)(2,1)S(1)}, u32[]{:S(2)}, u32[]{:S(2)}) collective-permute-start(bf16[1536,128]{1,0:T(8,128)(2,1)} %get-tuple-element.22), channel_id=1, source_target_pairs={{0,1},{1,2},{2,3},{3,0},{4,5},{5,6},{6,7},{7,4},{8,9},{9,10},{10,1... | collective-permute-start | bytes 1179656 | tf_op jit(solution)/shard_map/ppermute | solution.py:195
  70.3 20.5 %collective-permute-start.13 = (bf16[1536,128]{1,0:T(8,128)(2,1)}, bf16[1536,128]{1,0:T(8,128)(2,1)S(1)}, u32[]{:S(2)}, u32[]{:S(2)}) collective-permute-start(bf16[1536,128]{1,0:T(8,128)(2,1)} %get-tuple-element.23), channel_id=1, source_target_pairs={{0,2},{1,3},{2,0},{3,1},{4,6},{5,7},{6,4},{7,5},{8,10},{9,11},{10,... | collective-permute-start | bytes 1179656 | tf_op jit(solution)/shard_map/ppermute | solution.py:195
  73.1 18.0 %collective-permute-start.14 = (bf16[1536,128]{1,0:T(8,128)(2,1)}, bf16[1536,128]{1,0:T(8,128)(2,1)S(1)}, u32[]{:S(2)}, u32[]{:S(2)}) collective-permute-start(bf16[1536,128]{1,0:T(8,128)(2,1)} %get-tuple-element.24), channel_id=1, source_target_pairs={{0,3},{1,0},{2,1},{3,2},{4,7},{5,4},{6,5},{7,6},{8,11},{9,8},{10,9... | collective-permute-start | bytes 1179656 | tf_op jit(solution)/shard_map/ppermute | solution.py:195
  76.4 19.3 %all-to-all-start.1 = ((f32[32,16,128]{2,1,0:T(8,128)}), f32[32,16,128]{2,1,0:T(8,128)S(1)}, u32[]{:S(2)}, u32[]{:S(2)}) async-start(f32[32,16,128]{2,1,0:T(8,128)} %broadcast_in_dim.30), calls=%async_computation.1 | async-start | bytes 524288 | tf_op jit(solution)/shard_map/all_to_all | solution.py:228
  92.0 5.6 %collective-permute-start.15 = (bf16[256,128]{1,0:T(8,128)(2,1)S(1)}, bf16[256,128]{1,0:T(8,128)(2,1)S(1)}, u32[]{:S(2)}, u32[]{:S(2)}) collective-permute-start(bf16[256,128]{1,0:T(8,128)(2,1)S(1)} %get-tuple-element.30), channel_id=1, source_target_pairs={{0,112},{16,0},{32,16},{48,32},{64,48},{80,64},{96,80},{112,96},{1... | collective-permute-start | bytes 196616 | tf_op jit(solution)/shard_map/ppermute | solution.py:223
  95.7 6.4 %collective-permute-start.16 = (bf16[256,128]{1,0:T(8,128)(2,1)S(1)}, bf16[256,128]{1,0:T(8,128)(2,1)S(1)}, u32[]{:S(2)}, u32[]{:S(2)}) collective-permute-start(bf16[256,128]{1,0:T(8,128)(2,1)S(1)} %get-tuple-element.29), channel_id=1, source_target_pairs={{0,16},{16,32},{32,48},{48,64},{64,80},{80,96},{96,112},{112,0},{1... | collective-permute-start | bytes 196616 | tf_op jit(solution)/shard_map/ppermute | solution.py:224
  (5 other events, 7.2 us)

commit v3 on v2

--- a/solution.py
+++ b/solution.py
@@ -64,13 +64,16 @@
     )(inv, tile_values)
 
 
-def columns_kernel(depth, band, n0, n1, n2, n3, f0, f1, f2, f3, w0, w1, w2, w3, *refs):
+def columns_kernel(depth, band, own, zed, pair, f0, f1, f2, f3, w0, w1, w2, w3, *refs):
     parts, (acc, weight) = refs[0:4], refs[4:]
-    for s, w in enumerate((w0, w1, w2, w3)):
-        weight[:, s * T:(s + 1) * T] = w[8 * T:12 * T, :]
+    for t in range(4):
+        src = pl.ds(pl.multiple_of(8 * T + (depth[0] + t) % 4 * T, T), T)
+        for s, w in enumerate((w0, w1, w2, w3)):
+            weight[t * T:(t + 1) * T, s * T:(s + 1) * T] = w[src, :]
     acc[...] = jnp.zeros_like(acc)
     for q in range(QUADS):
-        sides = [jnp.concatenate([part[q * T:(q + 1) * T] for part in (n0, n1, n2, n3)], axis=0)]
+        here, later = slice(q * T, (q + 1) * T), slice((8 + q) * T, (9 + q) * T)
+        sides = [jnp.concatenate([own[here], pair[here], zed[here], pair[later]], axis=0)]
         for s in range(3):
             at = slice((8 * s + q) * T, (8 * s + q + 1) * T)
             sides.append(jnp.concatenate([part[at] for part in (f0, f1, f2, f3)], axis=0))
@@ -79,19 +82,17 @@
         )
     for k in range(6):
         rows = slice(k * 2 * T, (k + 1) * 2 * T)
-        spread = acc[rows, :].astype(bf16)
+        got = lax.dot_general(
+            acc[rows, :].astype(bf16), weight[...], (((1,), (1,)), ((), ())), preferred_element_type=f32
+        ).astype(bf16)
         for t in range(4):
-            src = pl.ds(pl.multiple_of((depth[0] + t) % 4 * T, T), T)
-            got = lax.dot_general(
-                spread, weight[src, :], (((1,), (1,)), ((), ())), preferred_element_type=f32
-            ).astype(bf16)
-            parts[t][rows, :] = got
+            parts[t][rows, :] = got[:, t * T:(t + 1) * T]
 
 
 def columns(depth, band, near, far, given):
     return pl.pallas_call(
         columns_kernel,
-        in_specs=[SMEM] + [VMEM] * 13,
+        in_specs=[SMEM] + [VMEM] * 12,
         out_specs=[VMEM] * 4,
         out_shape=[jax.ShapeDtypeStruct((12 * T, T), bf16)] * 4,
         scratch_shapes=[pltpu.VMEM((12 * T, 4 * T), f32), pltpu.VMEM((4 * T, 4 * T), bf16)],
@@ -196,20 +197,20 @@
 
     own = masked(out_grad, relu_mask, 0)
     zed = other(own)
-    near = (own, pair(own), zed, pair(zed))
+    near = (own, zed, pair(jnp.concatenate([own, zed], axis=0)))
     grads, mask = after((out_grad, relu_mask), own)
     rows = {t: from_depth(masked(grads, mask, t), t) for t in (2, 1, 3)}
 
     more = jnp.concatenate([rows[1], rows[2], rows[3]], axis=0)
     zed = other(after(more, zed))
-    late, late_weight = after((aggregated, weight), more)
+    late, late_weight = after((aggregated, weight), rows[1])
     given = [jnp.concatenate([quarter(late, t), late_weight], axis=0) for t in range(4)]
     given = given[:1] + [from_depth(given[t], t) for t in (1, 2, 3)]
     inv = inverse_table(tile_rows[0, 0], tile_cols[0, 0], tile_count[0, 0], stripe, col, depth)
     band = densify(after(inv, more), tile_values)
 
-    pieces = outer(depth1, given, own, more).reshape(128, 16, T)
-    far = (more, pair(more), zed, pair(after(zed, band, pieces)))
+    pieces = outer(after(depth1, band, near[2]), given, own, more).reshape(128, 16, T)
+    far = (more, pair(more), zed, pair(after(zed, pieces)))
     pieces = lax.all_to_all(pieces, ("row", "col", "depth"), 0, 0)
 
     res = columns(depth1, band, near, far, given)

time: 104 us -> 102 us (0.981)
  local copies, waits for them, and re-layouts: 8.83 us -> 7.44 us
  waiting for transfers between devices: 32 us -> 30.8 us
    all_to_all x1, starting transfers between devices: 6.06 us -> 9.87 us  [local(): pieces = lax.all_to_all(pieces, ('row', 'col', 'depth'), 0, 0)]
    ppermute x2, starting transfers between devices: 7.75 us -> 4.47 us  [other(): return lax.ppermute(array, 'col', flip(2))]
    ppermute x4 -> x3, waiting for transfers between devices: 1.61 us -> 0.01 us  [pair(): return lax.ppermute(array, 'col', flip(1))]
    unnamed x23 -> x19, local copies, waits for them, and re-layouts: 8 us -> 6.61 us
  transfers between devices with their start and end apart: 19 -> 18, of which waited for: 9 -> 6; matrix products, arithmetic and copies ran while one was open for 4% -> 6% of each run, Pallas kernels for 12% -> 12%
where the time goes in v3:
time: 102 us
  starting transfers between devices  42 us (41%)
  waiting for transfers between devices  30.8 us (30%)
  Pallas kernels  13.4 us (13%)
  local copies, waits for them, and re-layouts  7.44 us (7%)
  other arithmetic  6.35 us (6%)
  between operations  1.49 us (1%)
    ppermute x9, waiting for transfers between devices, from_depth(): return lax.ppermute(array, 'depth', ring(4, t))  24.5 us
    ppermute x9, starting transfers between devices, from_depth(): return lax.ppermute(array, 'depth', ring(4, t))  16.1 us
    all_to_all x1, starting transfers between devices, local(): pieces = lax.all_to_all(pieces, ('row', 'col', 'depth'), 0, 0)  9.87 us
    all_to_all x1, starting transfers between devices, local(): lax.all_to_all(jnp.broadcast_to(piece, (32, 16, T)), RC, 0, 0)  7.59 us
    unnamed x19, local copies, waits for them, and re-layouts  6.61 us
    pallas_call x1, Pallas kernels, columns(): pl.pallas_call(columns_kernel, in_specs=[SMEM] + [VMEM] * 12, out_specs=[...  6.32 us
    ppermute x1, waiting for transfers between devices, local(): lax.ppermute(of_quarter(3, slice(10 * T, 12 * T)), 'row', ring(8, 1))  4.47 us
    ppermute x2, starting transfers between devices, other(): return lax.ppermute(array, 'col', flip(2))  4.47 us
  transfers between devices with their start and end apart: 18, of which 6 were waited for; matrix products, arithmetic and copies ran while one was open for 6% of the time, Pallas kernels for 12%

profile of v3, /device:TPU:0, one launch (start us, length us, event | category | flops | bytes accessed | tf_op | source)
XLA Modules:
  0.0 101.5 jit_solution(11196940475195692489)
XLA Ops:
  0.6 1.2 %fusion.own = bf16[1024,128]{1,0:T(8,128)(2,1)S(1)} fusion(s32[4096,128]{1,0:T(8,128)} %param.9, s32[]{:T(128)S(6)} %select_n.182, bf16[4096,128]{1,0:T(8,128)(2,1)} %param.8), kind=kLoop, calls=%fused_computation.10 | loop fusion | flops 262144 | bytes 1048580 | tf_op jit(solution)/shard_map/jit(_where)/select_n | solution.py:193
  1.8 4.0 %collective-permute-start.3 = (bf16[1024,128]{1,0:T(8,128)(2,1)S(1)}, bf16[1024,128]{1,0:T(8,128)(2,1)S(1)}, u32[]{:S(2)}, u32[]{:S(2)}) collective-permute-start(bf16[1024,128]{1,0:T(8,128)(2,1)S(1)} %fusion.own), channel_id=1, source_target_pairs={{0,8},{4,12},{8,0},{12,4},{1,9},{5,13},{9,1},{13,5},{2,10},{6,14},... | collective-permute-start | bytes 786440 | tf_op jit(solution)/shard_map/ppermute | solution.py:182
  5.9 1.8 %fusion.3 = (bf16[1024,128]{1,0:T(8,128)(2,1)S(1)}, bf16[1024,128]{1,0:T(8,128)(2,1)S(1)}, bf16[1024,128]{1,0:T(8,128)(2,1)S(1)}) fusion(s32[4096,128]{1,0:T(8,128)} %param.9, s32[]{:T(128)S(6)} %select_n.191, bf16[4096,128]{1,0:T(8,128)(2,1)} %param.8, s32[]{:T(128)S(6)} %select_n.188, s32[]{:T(128)S(6)} %select_n.185), kind=kLoop, calls=%fused_computation.13 | loop fusion | flops 786432 | bytes 3145740 | tf_op jit(solution)/shard_map/jit(_where)/select_n | solution.py:193
  7.7 1.6 %collective-permute-start = (bf16[1024,128]{1,0:T(8,128)(2,1)S(1)}, bf16[1024,128]{1,0:T(8,128)(2,1)S(1)}, u32[]{:S(2)}, u32[]{:S(2)}) collective-permute-start(bf16[1024,128]{1,0:T(8,128)(2,1)S(1)} %get-tuple-element.30), channel_id=1, source_target_pairs={{0,1},{1,2},{2,3},{3,0},{4,5},{5,6},{6,7},{7,4},{8,9},{9,10},{10,1... | collective-permute-start | bytes 786440 | tf_op jit(solution)/shard_map/ppermute | solution.py:196
  9.3 2.9 %collective-permute-start.1 = (bf16[1024,128]{1,0:T(8,128)(2,1)S(1)}, bf16[1024,128]{1,0:T(8,128)(2,1)S(1)}, u32[]{:S(2)}, u32[]{:S(2)}) collective-permute-start(bf16[1024,128]{1,0:T(8,128)(2,1)S(1)} %get-tuple-element.29), channel_id=1, source_target_pairs={{0,2},{1,3},{2,0},{3,1},{4,6},{5,7},{6,4},{7,5},{8,10},{9,11},{10,... | collective-permute-start | bytes 786440 | tf_op jit(solution)/shard_map/ppermute | solution.py:196
  12.2 1.3 %collective-permute-start.2 = (bf16[1024,128]{1,0:T(8,128)(2,1)S(1)}, bf16[1024,128]{1,0:T(8,128)(2,1)S(1)}, u32[]{:S(2)}, u32[]{:S(2)}) collective-permute-start(bf16[1024,128]{1,0:T(8,128)(2,1)S(1)} %get-tuple-element.28), channel_id=1, source_target_pairs={{0,3},{1,0},{2,1},{3,2},{4,7},{5,4},{6,5},{7,6},{8,11},{9,8},{10,9... | collective-permute-start | bytes 786440 | tf_op jit(solution)/shard_map/ppermute | solution.py:196
  14.4 2.7 %collective-permute-done = bf16[1024,128]{1,0:T(8,128)(2,1)S(1)} collective-permute-done((bf16[1024,128]{1,0:T(8,128)(2,1)S(1)}, bf16[1024,128]{1,0:T(8,128)(2,1)S(1)}, u32[]{:S(2)}, u32[]{:S(2)}) %collective-permute-start) | collective-permute-done | bytes 262176 | tf_op jit(solution)/shard_map/ppermute | solution.py:196
  17.1 6.5 %collective-permute-done.1 = bf16[1024,128]{1,0:T(8,128)(2,1)S(1)} collective-permute-done((bf16[1024,128]{1,0:T(8,128)(2,1)S(1)}, bf16[1024,128]{1,0:T(8,128)(2,1)S(1)}, u32[]{:S(2)}, u32[]{:S(2)}) %collective-permute-start.1) | collective-permute-done | bytes 262176 | tf_op jit(solution)/shard_map/ppermute | solution.py:196
  26.5 2.4 %collective-permute-start.8 = (bf16[1536,128]{1,0:T(8,128)(2,1)}, bf16[1536,128]{1,0:T(8,128)(2,1)S(1)}, u32[]{:S(2)}, u32[]{:S(2)}) collective-permute-start(bf16[1536,128]{1,0:T(8,128)(2,1)} %get-tuple-element.39), channel_id=1, source_target_pairs={{0,2},{1,3},{2,0},{3,1},{4,6},{5,7},{6,4},{7,5},{8,10},{9,11},{10,... | collective-permute-start | bytes 1179656 | tf_op jit(solution)/shard_map/ppermute | solution.py:196
  28.9 1.6 %collective-permute-start.9 = (bf16[1536,128]{1,0:T(8,128)(2,1)}, bf16[1536,128]{1,0:T(8,128)(2,1)S(1)}, u32[]{:S(2)}, u32[]{:S(2)}) collective-permute-start(bf16[1536,128]{1,0:T(8,128)(2,1)} %get-tuple-element.37), channel_id=1, source_target_pairs={{0,3},{1,0},{2,1},{3,2},{4,7},{5,4},{6,5},{7,6},{8,11},{9,8},{10,9... | collective-permute-start | bytes 1179656 | tf_op jit(solution)/shard_map/ppermute | solution.py:196
  31.4 4.1 %densify.1.band = bf16[8,640,512]{2,1,0:T(8,128)(2,1)S(1)} custom-call(s32[160]{0:T(256)S(1)} %select_reduce_fusion.inv, bf16[1,1,544,128,128]{4,3,2,1,0:T(8,128)(2,1)} %tiles.1), custom_call_target="tpu_custom_call" | custom-call | flops 1024 | bytes 1024 | tf_op jit(solution)/shard_map/densify/pallas_call | solution.py:55
  35.5 2.3 %copy-done = bf16[8,640,512]{2,1,0:T(8,128)(2,1)} copy-done((bf16[8,640,512]{2,1,0:T(8,128)(2,1)}, bf16[8,640,512]{2,1,0:T(8,128)(2,1)S(1)}, u32[]{:S(2)}) %copy-start) | copy-done | bytes 5242904
  37.8 8.4 %collective-permute-done.8.g2.w2 = bf16[1536,128]{1,0:T(8,128)(2,1)S(1)} collective-permute-done((bf16[1536,128]{1,0:T(8,128)(2,1)}, bf16[1536,128]{1,0:T(8,128)(2,1)S(1)}, u32[]{:S(2)}, u32[]{:S(2)}) %collective-permute-start.8) | collective-permute-done | bytes 393248 | tf_op jit(solution)/shard_map/ppermute | solution.py:196
  46.3 1.8 %outer.1 = bf16[32,4,16,128]{3,2,1,0:T(8,128)(2,1)} custom-call(s32[1]{0:T(128)} %bitcast.depth, bf16[1536,128]{1,0:T(8,128)(2,1)S(1)} %get-tuple-element.40.g0.w0, bf16[1536,128]{1,0:T(8,128)(2,1)S(1)} %collective-permute-done.7.g1.w1, bf16[1536,128]{1,0:T(8,128)(2,1)S(1)} %collective-permute-done.8.g2.w2, ...), custom_call_target="tpu_custom_call" | custom-call | flops 1024 | bytes 1024 | tf_op jit(solution)/shard_map/outer/pallas_call | solution.py:148
  48.1 9.9 %all-to-all-start = ((bf16[128,16,128]{2,1,0:T(8,128)(2,1)}), bf16[128,16,128]{2,1,0:T(8,128)(2,1)}, u32[]{:S(2)}, u32[]{:S(2)}) async-start(bf16[128,16,128]{2,1,0:T(8,128)(2,1)} %bitcast.2), calls=%async_computation | async-start | bytes 1048576 | tf_op jit(solution)/shard_map/all_to_all | solution.py:214
  58.0 2.5 %copy-done.1 = bf16[8,640,512]{2,1,0:T(8,128)(2,1)S(1)} copy-done((bf16[8,640,512]{2,1,0:T(8,128)(2,1)S(1)}, bf16[8,640,512]{2,1,0:T(8,128)(2,1)}, u32[]{:S(2)}) %copy-start.1) | copy-done | bytes 5242904
  61.5 6.3 %columns.1 = (bf16[1536,128]{1,0:T(8,128)(2,1)S(1)}, bf16[1536,128]{1,0:T(8,128)(2,1)}, bf16[1536,128]{1,0:T(8,128)(2,1)}, bf16[1536,128]{1,0:T(8,128)(2,1)}) custom-call(s32[1]{0:T(128)} %bitcast.depth, bf16[8,640,512]{2,1,0:T(8,128)(2,1)S(1)} %copy-done.1, bf16[1024,128]{1,0:T(8,128)(2,1)S(1)} %fusion.own, ...), custom_call_target="tpu_custom_call" | custom-call | flops 1024 | bytes 1024 | tf_op jit(solution)/shard_map/columns/pallas_call | solution.py:93
  68.8 2.7 %collective-permute-start.12 = (bf16[1536,128]{1,0:T(8,128)(2,1)}, bf16[1536,128]{1,0:T(8,128)(2,1)S(1)}, u32[]{:S(2)}, u32[]{:S(2)}) collective-permute-start(bf16[1536,128]{1,0:T(8,128)(2,1)} %get-tuple-element.25), channel_id=1, source_target_pairs={{0,2},{1,3},{2,0},{3,1},{4,6},{5,7},{6,4},{7,5},{8,10},{9,11},{10,... | collective-permute-start | bytes 1179656 | tf_op jit(solution)/shard_map/ppermute | solution.py:196
  71.5 1.4 %collective-permute-start.13 = (bf16[1536,128]{1,0:T(8,128)(2,1)}, bf16[1536,128]{1,0:T(8,128)(2,1)S(1)}, u32[]{:S(2)}, u32[]{:S(2)}) collective-permute-start(bf16[1536,128]{1,0:T(8,128)(2,1)} %get-tuple-element.26), channel_id=1, source_target_pairs={{0,3},{1,0},{2,1},{3,2},{4,7},{5,4},{6,5},{7,6},{8,11},{9,8},{10,9... | collective-permute-start | bytes 1179656 | tf_op jit(solution)/shard_map/ppermute | solution.py:196
  74.8 7.6 %all-to-all-start.1 = ((f32[32,16,128]{2,1,0:T(8,128)}), f32[32,16,128]{2,1,0:T(8,128)S(1)}, u32[]{:S(2)}, u32[]{:S(2)}) async-start(f32[32,16,128]{2,1,0:T(8,128)} %broadcast_in_dim.30), calls=%async_computation.1 | async-start | bytes 524288 | tf_op jit(solution)/shard_map/all_to_all | solution.py:229
  82.4 6.9 %collective-permute-done.12.r2 = bf16[1536,128]{1,0:T(8,128)(2,1)S(1)} collective-permute-done((bf16[1536,128]{1,0:T(8,128)(2,1)}, bf16[1536,128]{1,0:T(8,128)(2,1)S(1)}, u32[]{:S(2)}, u32[]{:S(2)}) %collective-permute-start.12) | collective-permute-done | bytes 393248 | tf_op jit(solution)/shard_map/ppermute | solution.py:196
  89.3 4.0 %collective-permute-start.14 = (bf16[256,128]{1,0:T(8,128)(2,1)S(1)}, bf16[256,128]{1,0:T(8,128)(2,1)S(1)}, u32[]{:S(2)}, u32[]{:S(2)}) collective-permute-start(bf16[256,128]{1,0:T(8,128)(2,1)S(1)} %get-tuple-element.32), channel_id=1, source_target_pairs={{0,112},{16,0},{32,16},{48,32},{64,48},{80,64},{96,80},{112,96},{1... | collective-permute-start | bytes 196616 | tf_op jit(solution)/shard_map/ppermute | solution.py:224
  93.3 1.9 %collective-permute-done.14.following = bf16[256,128]{1,0:T(8,128)(2,1)S(1)} collective-permute-done((bf16[256,128]{1,0:T(8,128)(2,1)S(1)}, bf16[256,128]{1,0:T(8,128)(2,1)S(1)}, u32[]{:S(2)}, u32[]{:S(2)}) %collective-permute-start.14) | collective-permute-done | bytes 65568 | tf_op jit(solution)/shard_map/ppermute | solution.py:224
  95.2 4.5 %collective-permute-done.15.previous = bf16[256,128]{1,0:T(8,128)(2,1)S(1)} collective-permute-done((bf16[256,128]{1,0:T(8,128)(2,1)S(1)}, bf16[256,128]{1,0:T(8,128)(2,1)S(1)}, u32[]{:S(2)}, u32[]{:S(2)}) %collective-permute-start.15) | collective-permute-done | bytes 65568 | tf_op jit(solution)/shard_map/ppermute | solution.py:225
  (48 shorter events, 9.8 us)
Async XLA Ops:
  1.8 11.7 %collective-permute-start.3 = (bf16[1024,128]{1,0:T(8,128)(2,1)S(1)}, bf16[1024,128]{1,0:T(8,128)(2,1)S(1)}, u32[]{:S(2)}, u32[]{:S(2)}) collective-permute-start(bf16[1024,128]{1,0:T(8,128)(2,1)S(1)} %fusion.own), channel_id=1, source_target_pairs={{0,8},{4,12},{8,0},{12,4},{1,9},{5,13},{9,1},{13,5},{2,10},{6,14},... | collective-permute-start | bytes 786440 | tf_op jit(solution)/shard_map/ppermute | solution.py:182
  7.7 16.5 %copy-start.4 = (bf16[4096,128]{1,0:T(8,128)(2,1)S(1)}, bf16[4096,128]{1,0:T(8,128)(2,1)}, u32[]{:S(2)}) copy-start(bf16[4096,128]{1,0:T(8,128)(2,1)} %param.10) | copy-start | bytes 3145732
  7.7 9.4 %collective-permute-start = (bf16[1024,128]{1,0:T(8,128)(2,1)S(1)}, bf16[1024,128]{1,0:T(8,128)(2,1)S(1)}, u32[]{:S(2)}, u32[]{:S(2)}) collective-permute-start(bf16[1024,128]{1,0:T(8,128)(2,1)S(1)} %get-tuple-element.30), channel_id=1, source_target_pairs={{0,1},{1,2},{2,3},{3,0},{4,5},{5,6},{6,7},{7,4},{8,9},{9,10},{10,1... | collective-permute-start | bytes 786440 | tf_op jit(solution)/shard_map/ppermute | solution.py:196
  9.3 14.3 %collective-permute-start.1 = (bf16[1024,128]{1,0:T(8,128)(2,1)S(1)}, bf16[1024,128]{1,0:T(8,128)(2,1)S(1)}, u32[]{:S(2)}, u32[]{:S(2)}) collective-permute-start(bf16[1024,128]{1,0:T(8,128)(2,1)S(1)} %get-tuple-element.29), channel_id=1, source_target_pairs={{0,2},{1,3},{2,0},{3,1},{4,6},{5,7},{6,4},{7,5},{8,10},{9,11},{10,... | collective-permute-start | bytes 786440 | tf_op jit(solution)/shard_map/ppermute | solution.py:196
  12.2 11.4 %collective-permute-start.2 = (bf16[1024,128]{1,0:T(8,128)(2,1)S(1)}, bf16[1024,128]{1,0:T(8,128)(2,1)S(1)}, u32[]{:S(2)}, u32[]{:S(2)}) collective-permute-start(bf16[1024,128]{1,0:T(8,128)(2,1)S(1)} %get-tuple-element.28), channel_id=1, source_target_pairs={{0,3},{1,0},{2,1},{3,2},{4,7},{5,4},{6,5},{7,6},{8,11},{9,8},{10,9... | collective-permute-start | bytes 786440 | tf_op jit(solution)/shard_map/ppermute | solution.py:196
  14.4 9.8 %copy-start.5 = (bf16[512,128]{1,0:T(8,128)(2,1)S(1)}, bf16[512,128]{1,0:T(8,128)(2,1)}, u32[]{:S(2)}) copy-start(bf16[512,128]{1,0:T(8,128)(2,1)} %param.11) | copy-start | bytes 393220
  17.1 20.8 %collective-permute-start.4 = (bf16[2048,128]{1,0:T(8,128)(2,1)}, bf16[2048,128]{1,0:T(8,128)(2,1)S(1)}, u32[]{:S(2)}, u32[]{:S(2)}) collective-permute-start(bf16[2048,128]{1,0:T(8,128)(2,1)} %pad_maximum_fusion.4), channel_id=1, source_target_pairs={{0,4},{4,0},{8,12},{12,8},{1,5},{5,1},{9,13},{13,9},{2,6},{6,2},{1... | collective-permute-start | bytes 1572872 | tf_op jit(solution)/shard_map/ppermute | solution.py:185
  23.7 6.8 %copy-start.6 = (s32[1,1,544]{2,1,0:T(1,128)S(1)}, s32[1,1,544]{2,1,0:T(1,128)}, u32[]{:S(2)}) copy-start(s32[1,1,544]{2,1,0:T(1,128)} %param.13) | copy-start | bytes 6532
  23.7 6.8 %copy-start.7 = (s32[1,1,544]{2,1,0:T(1,128)S(1)}, s32[1,1,544]{2,1,0:T(1,128)}, u32[]{:S(2)}) copy-start(s32[1,1,544]{2,1,0:T(1,128)} %param.14) | copy-start | bytes 6532
  23.7 24.4 %collective-permute-start.6 = (bf16[3072,128]{1,0:T(8,128)(2,1)S(1)}, bf16[3072,128]{1,0:T(8,128)(2,1)}, u32[]{:S(2)}, u32[]{:S(2)}) collective-permute-start(bf16[3072,128]{1,0:T(8,128)(2,1)S(1)} %constant_dynamic-update-slice_fusion.more.f0), channel_id=1, source_target_pairs={{0,8},{4,12},{8,0},{12,4},{1,9},{5,13},{9,1},{13,5},{2,10},{6,14},... | collective-permute-start | bytes 2359304 | tf_op jit(solution)/shard_map/ppermute | solution.py:182
  25.4 12.5 %collective-permute-start.7 = (bf16[1536,128]{1,0:T(8,128)(2,1)}, bf16[1536,128]{1,0:T(8,128)(2,1)S(1)}, u32[]{:S(2)}, u32[]{:S(2)}) collective-permute-start(bf16[1536,128]{1,0:T(8,128)(2,1)} %get-tuple-element.38), channel_id=1, source_target_pairs={{0,1},{1,2},{2,3},{3,0},{4,5},{5,6},{6,7},{7,4},{8,9},{9,10},{10,1... | collective-permute-start | bytes 1179656 | tf_op jit(solution)/shard_map/ppermute | solution.py:196
  26.5 19.8 %collective-permute-start.8 = (bf16[1536,128]{1,0:T(8,128)(2,1)}, bf16[1536,128]{1,0:T(8,128)(2,1)S(1)}, u32[]{:S(2)}, u32[]{:S(2)}) collective-permute-start(bf16[1536,128]{1,0:T(8,128)(2,1)} %get-tuple-element.39), channel_id=1, source_target_pairs={{0,2},{1,3},{2,0},{3,1},{4,6},{5,7},{6,4},{7,5},{8,10},{9,11},{10,... | collective-permute-start | bytes 1179656 | tf_op jit(solution)/shard_map/ppermute | solution.py:196
  28.9 17.4 %collective-permute-start.9 = (bf16[1536,128]{1,0:T(8,128)(2,1)}, bf16[1536,128]{1,0:T(8,128)(2,1)S(1)}, u32[]{:S(2)}, u32[]{:S(2)}) collective-permute-start(bf16[1536,128]{1,0:T(8,128)(2,1)} %get-tuple-element.37), channel_id=1, source_target_pairs={{0,3},{1,0},{2,1},{3,2},{4,7},{5,4},{6,5},{7,6},{8,11},{9,8},{10,9... | collective-permute-start | bytes 1179656 | tf_op jit(solution)/shard_map/ppermute | solution.py:196
  37.8 10.3 %copy-start.2 = (bf16[2048,128]{1,0:T(8,128)(2,1)}, bf16[2048,128]{1,0:T(8,128)(2,1)S(1)}, u32[]{:S(2)}) copy-start(bf16[2048,128]{1,0:T(8,128)(2,1)S(1)} %collective-permute-done.4.pair) | copy-start | bytes 1572868
  37.8 20.2 %collective-permute-start.5 = (bf16[3072,128]{1,0:T(8,128)(2,1)S(1)}, bf16[3072,128]{1,0:T(8,128)(2,1)}, u32[]{:S(2)}, u32[]{:S(2)}) collective-permute-start(bf16[3072,128]{1,0:T(8,128)(2,1)S(1)} %constant_dynamic-update-slice_fusion.more.f0), channel_id=1, source_target_pairs={{0,4},{4,0},{8,12},{12,8},{1,5},{5,1},{9,13},{13,9},{2,6},{6,2},{1... | collective-permute-start | bytes 2359304 | tf_op jit(solution)/shard_map/ppermute | solution.py:185
  48.1 9.9 %collective-permute-start.10 = (bf16[3072,128]{1,0:T(8,128)(2,1)}, bf16[3072,128]{1,0:T(8,128)(2,1)}, u32[]{:S(2)}, u32[]{:S(2)}) collective-permute-start(bf16[3072,128]{1,0:T(8,128)(2,1)} %collective-permute-done.6.f2), channel_id=1, source_target_pairs={{0,4},{4,0},{8,12},{12,8},{1,5},{5,1},{9,13},{13,9},{2,6},{6,2},{1... | collective-permute-start | bytes 2359304 | tf_op jit(solution)/shard_map/ppermute | solution.py:185
  48.1 24.8 %all-to-all-start = ((bf16[128,16,128]{2,1,0:T(8,128)(2,1)}), bf16[128,16,128]{2,1,0:T(8,128)(2,1)}, u32[]{:S(2)}, u32[]{:S(2)}) async-start(bf16[128,16,128]{2,1,0:T(8,128)(2,1)} %bitcast.2), calls=%async_computation | async-start | bytes 1048576 | tf_op jit(solution)/shard_map/all_to_all | solution.py:214
  58.0 2.5 %copy-start.1 = (bf16[8,640,512]{2,1,0:T(8,128)(2,1)S(1)}, bf16[8,640,512]{2,1,0:T(8,128)(2,1)}, u32[]{:S(2)}) copy-start(bf16[8,640,512]{2,1,0:T(8,128)(2,1)} %copy-done) | copy-start | bytes 15728644
  67.9 14.5 %collective-permute-start.11 = (bf16[1536,128]{1,0:T(8,128)(2,1)}, bf16[1536,128]{1,0:T(8,128)(2,1)S(1)}, u32[]{:S(2)}, u32[]{:S(2)}) collective-permute-start(bf16[1536,128]{1,0:T(8,128)(2,1)} %get-tuple-element.24), channel_id=1, source_target_pairs={{0,1},{1,2},{2,3},{3,0},{4,5},{5,6},{6,7},{7,4},{8,9},{9,10},{10,1... | collective-permute-start | bytes 1179656 | tf_op jit(solution)/shard_map/ppermute | solution.py:196
  68.8 20.5 %collective-permute-start.12 = (bf16[1536,128]{1,0:T(8,128)(2,1)}, bf16[1536,128]{1,0:T(8,128)(2,1)S(1)}, u32[]{:S(2)}, u32[]{:S(2)}) collective-permute-start(bf16[1536,128]{1,0:T(8,128)(2,1)} %get-tuple-element.25), channel_id=1, source_target_pairs={{0,2},{1,3},{2,0},{3,1},{4,6},{5,7},{6,4},{7,5},{8,10},{9,11},{10,... | collective-permute-start | bytes 1179656 | tf_op jit(solution)/shard_map/ppermute | solution.py:196
  71.5 17.8 %collective-permute-start.13 = (bf16[1536,128]{1,0:T(8,128)(2,1)}, bf16[1536,128]{1,0:T(8,128)(2,1)S(1)}, u32[]{:S(2)}, u32[]{:S(2)}) collective-permute-start(bf16[1536,128]{1,0:T(8,128)(2,1)} %get-tuple-element.26), channel_id=1, source_target_pairs={{0,3},{1,0},{2,1},{3,2},{4,7},{5,4},{6,5},{7,6},{8,11},{9,8},{10,9... | collective-permute-start | bytes 1179656 | tf_op jit(solution)/shard_map/ppermute | solution.py:196
  74.8 18.5 %all-to-all-start.1 = ((f32[32,16,128]{2,1,0:T(8,128)}), f32[32,16,128]{2,1,0:T(8,128)S(1)}, u32[]{:S(2)}, u32[]{:S(2)}) async-start(f32[32,16,128]{2,1,0:T(8,128)} %broadcast_in_dim.30), calls=%async_computation.1 | async-start | bytes 524288 | tf_op jit(solution)/shard_map/all_to_all | solution.py:229
  89.3 5.9 %collective-permute-start.14 = (bf16[256,128]{1,0:T(8,128)(2,1)S(1)}, bf16[256,128]{1,0:T(8,128)(2,1)S(1)}, u32[]{:S(2)}, u32[]{:S(2)}) collective-permute-start(bf16[256,128]{1,0:T(8,128)(2,1)S(1)} %get-tuple-element.32), channel_id=1, source_target_pairs={{0,112},{16,0},{32,16},{48,32},{64,48},{80,64},{96,80},{112,96},{1... | collective-permute-start | bytes 196616 | tf_op jit(solution)/shard_map/ppermute | solution.py:224
  93.3 6.4 %collective-permute-start.15 = (bf16[256,128]{1,0:T(8,128)(2,1)S(1)}, bf16[256,128]{1,0:T(8,128)(2,1)S(1)}, u32[]{:S(2)}, u32[]{:S(2)}) collective-permute-start(bf16[256,128]{1,0:T(8,128)(2,1)S(1)} %get-tuple-element.31), channel_id=1, source_target_pairs={{0,16},{16,32},{32,48},{48,64},{64,80},{80,96},{96,112},{112,0},{1... | collective-permute-start | bytes 196616 | tf_op jit(solution)/shard_map/ppermute | solution.py:225
  (2 other events, 3.4 us)

commit v4 on v3

--- a/solution.py
+++ b/solution.py
@@ -70,16 +70,17 @@
         src = pl.ds(pl.multiple_of(8 * T + (depth[0] + t) % 4 * T, T), T)
         for s, w in enumerate((w0, w1, w2, w3)):
             weight[t * T:(t + 1) * T, s * T:(s + 1) * T] = w[src, :]
-    acc[...] = jnp.zeros_like(acc)
     for q in range(QUADS):
         here, later = slice(q * T, (q + 1) * T), slice((8 + q) * T, (9 + q) * T)
         sides = [jnp.concatenate([own[here], pair[here], zed[here], pair[later]], axis=0)]
         for s in range(3):
             at = slice((8 * s + q) * T, (8 * s + q + 1) * T)
             sides.append(jnp.concatenate([part[at] for part in (f0, f1, f2, f3)], axis=0))
-        acc[q * T:(q + SLOTS) * T, :] += jnp.dot(
-            band[q], jnp.concatenate(sides, axis=1), preferred_element_type=f32
-        )
+        got = jnp.dot(band[q], jnp.concatenate(sides, axis=1), preferred_element_type=f32)
+        seen = 0 if q == 0 else SLOTS - 1
+        if seen:
+            acc[q * T:(q + seen) * T, :] += got[0:seen * T]
+        acc[(q + seen) * T:(q + SLOTS) * T, :] = got[seen * T:SLOTS * T]
     for k in range(6):
         rows = slice(k * 2 * T, (k + 1) * 2 * T)
         got = lax.dot_general(
@@ -102,7 +103,8 @@
     )(depth, band, *near, *far, *given)
 
 
-def place_kernel(depth, r0, r1, r2, r3, following, previous, out, ends):
+def place_kernel(depth, r0, r1, r2, r3, following, previous, grad_weight, out, out_weight, ends):
+    out_weight[...] = grad_weight[...]
     ends[0, 2 * T:4 * T] = previous[...]
     ends[5, 0:2 * T] = following[...]
     for t, part in enumerate((r0, r1, r2, r3)):
@@ -118,17 +120,20 @@
         out[k, 6 * T:8 * T] = (part[8 * T:10 * T, :].astype(f32) + behind).astype(bf16)
 
 
-def place(depth, parts, following, previous):
+def place(depth, parts, following, previous, grad_weight):
     return pl.pallas_call(
         place_kernel,
-        in_specs=[SMEM] + [VMEM] * 6,
-        out_specs=VMEM,
-        out_shape=jax.ShapeDtypeStruct((4, 8 * T, T), bf16),
+        in_specs=[SMEM] + [VMEM] * 7,
+        out_specs=[VMEM] * 2,
+        out_shape=[
+            jax.ShapeDtypeStruct((4, 8 * T, T), bf16),
+            jax.ShapeDtypeStruct((4 * T, T), f32),
+        ],
         scratch_shapes=[pltpu.VMEM((6, 4 * T, T), bf16)],
         compiler_params=params(8),
         cost_estimate=SMALL,
         name="place",
-    )(depth, *parts, following, previous)
+    )(depth, *parts, following, previous, grad_weight)
 
 
 def outer_kernel(depth, g0, g1, g2, g3, own, more, out, turned):
@@ -223,11 +228,11 @@
 
     following = lax.ppermute(of_quarter(0, slice(0, 2 * T)), "row", ring(8, -1))
     previous = lax.ppermute(of_quarter(3, slice(10 * T, 12 * T)), "row", ring(8, 1))
-    grad_input = place(depth1, back, following, previous).reshape(32 * T, T)
 
     piece = jnp.sum(after(pieces, res[0]).astype(f32), axis=0)
     grad_weight = lax.all_to_all(jnp.broadcast_to(piece, (32, 16, T)), RC, 0, 0).reshape(4 * T, T)
-    return grad_input, grad_weight
+    grad_input, grad_weight = place(depth1, back, following, previous, grad_weight)
+    return grad_input.reshape(32 * T, T), grad_weight
 
 
 def solution(mesh):

time: 102 us -> 101 us (level)
    unnamed x19 -> x18, local copies, waits for them, and re-layouts: 6.61 us -> 5.92 us
where the time goes in v4:
time: 101 us
  starting transfers between devices  42 us (42%)
  waiting for transfers between devices  30.7 us (30%)
  Pallas kernels  13.6 us (13%)
  local copies, waits for them, and re-layouts  6.75 us (7%)
  other arithmetic  6.33 us (6%)
  between operations  1.49 us (1%)
    ppermute x9, waiting for transfers between devices, from_depth(): return lax.ppermute(array, 'depth', ring(4, t))  24.3 us
    ppermute x9, starting transfers between devices, from_depth(): return lax.ppermute(array, 'depth', ring(4, t))  16.1 us
    all_to_all x1, starting transfers between devices, local(): pieces = lax.all_to_all(pieces, ('row', 'col', 'depth'), 0, 0)  9.88 us
    all_to_all x1, starting transfers between devices, local(): lax.all_to_all(jnp.broadcast_to(piece, (32, 16, T)), RC, 0, 0)  7.59 us
    pallas_call x1, Pallas kernels, columns(): pl.pallas_call(columns_kernel, in_specs=[SMEM] + [VMEM] * 12, out_specs=[...  6.33 us
    unnamed x18, local copies, waits for them, and re-layouts  5.92 us
    ppermute x1, waiting for transfers between devices, local(): lax.ppermute(of_quarter(3, slice(10 * T, 12 * T)), 'row', ring(8, 1))  4.47 us
    ppermute x2, starting transfers between devices, other(): return lax.ppermute(array, 'col', flip(2))  4.47 us
  transfers between devices with their start and end apart: 18, of which 6 were waited for; matrix products, arithmetic and copies ran while one was open for 6% of the time, Pallas kernels for 12%

profile of v4, /device:TPU:0, one launch (start us, length us, event | category | flops | bytes accessed | tf_op | source)
XLA Modules:
  0.0 100.8 jit_solution(10714102801658522002)
XLA Ops:
  1.8 4.0 %collective-permute-start.3 = (bf16[1024,128]{1,0:T(8,128)(2,1)S(1)}, bf16[1024,128]{1,0:T(8,128)(2,1)S(1)}, u32[]{:S(2)}, u32[]{:S(2)}) collective-permute-start(bf16[1024,128]{1,0:T(8,128)(2,1)S(1)} %fusion.own), channel_id=1, source_target_pairs={{0,8},{4,12},{8,0},{12,4},{1,9},{5,13},{9,1},{13,5},{2,10},{6,14},... | collective-permute-start | bytes 786440 | tf_op jit(solution)/shard_map/ppermute | solution.py:187
  5.9 1.8 %fusion.3 = (bf16[1024,128]{1,0:T(8,128)(2,1)S(1)}, bf16[1024,128]{1,0:T(8,128)(2,1)S(1)}, bf16[1024,128]{1,0:T(8,128)(2,1)S(1)}) fusion(s32[4096,128]{1,0:T(8,128)} %param.9, s32[]{:T(128)S(6)} %select_n.191, bf16[4096,128]{1,0:T(8,128)(2,1)} %param.8, s32[]{:T(128)S(6)} %select_n.188, s32[]{:T(128)S(6)} %select_n.185), kind=kLoop, calls=%fused_computation.13 | loop fusion | flops 786432 | bytes 3145740 | tf_op jit(solution)/shard_map/jit(_where)/select_n | solution.py:198
  7.7 1.6 %collective-permute-start = (bf16[1024,128]{1,0:T(8,128)(2,1)S(1)}, bf16[1024,128]{1,0:T(8,128)(2,1)S(1)}, u32[]{:S(2)}, u32[]{:S(2)}) collective-permute-start(bf16[1024,128]{1,0:T(8,128)(2,1)S(1)} %get-tuple-element.34), channel_id=1, source_target_pairs={{0,1},{1,2},{2,3},{3,0},{4,5},{5,6},{6,7},{7,4},{8,9},{9,10},{10,1... | collective-permute-start | bytes 786440 | tf_op jit(solution)/shard_map/ppermute | solution.py:201
  9.3 2.9 %collective-permute-start.1 = (bf16[1024,128]{1,0:T(8,128)(2,1)S(1)}, bf16[1024,128]{1,0:T(8,128)(2,1)S(1)}, u32[]{:S(2)}, u32[]{:S(2)}) collective-permute-start(bf16[1024,128]{1,0:T(8,128)(2,1)S(1)} %get-tuple-element.33), channel_id=1, source_target_pairs={{0,2},{1,3},{2,0},{3,1},{4,6},{5,7},{6,4},{7,5},{8,10},{9,11},{10,... | collective-permute-start | bytes 786440 | tf_op jit(solution)/shard_map/ppermute | solution.py:201
  12.2 1.3 %collective-permute-start.2 = (bf16[1024,128]{1,0:T(8,128)(2,1)S(1)}, bf16[1024,128]{1,0:T(8,128)(2,1)S(1)}, u32[]{:S(2)}, u32[]{:S(2)}) collective-permute-start(bf16[1024,128]{1,0:T(8,128)(2,1)S(1)} %get-tuple-element.32), channel_id=1, source_target_pairs={{0,3},{1,0},{2,1},{3,2},{4,7},{5,4},{6,5},{7,6},{8,11},{9,8},{10,9... | collective-permute-start | bytes 786440 | tf_op jit(solution)/shard_map/ppermute | solution.py:201
  14.4 2.7 %collective-permute-done = bf16[1024,128]{1,0:T(8,128)(2,1)S(1)} collective-permute-done((bf16[1024,128]{1,0:T(8,128)(2,1)S(1)}, bf16[1024,128]{1,0:T(8,128)(2,1)S(1)}, u32[]{:S(2)}, u32[]{:S(2)}) %collective-permute-start) | collective-permute-done | bytes 262176 | tf_op jit(solution)/shard_map/ppermute | solution.py:201
  17.1 6.5 %collective-permute-done.1 = bf16[1024,128]{1,0:T(8,128)(2,1)S(1)} collective-permute-done((bf16[1024,128]{1,0:T(8,128)(2,1)S(1)}, bf16[1024,128]{1,0:T(8,128)(2,1)S(1)}, u32[]{:S(2)}, u32[]{:S(2)}) %collective-permute-start.1) | collective-permute-done | bytes 262176 | tf_op jit(solution)/shard_map/ppermute | solution.py:201
  26.5 2.4 %collective-permute-start.8 = (bf16[1536,128]{1,0:T(8,128)(2,1)}, bf16[1536,128]{1,0:T(8,128)(2,1)S(1)}, u32[]{:S(2)}, u32[]{:S(2)}) collective-permute-start(bf16[1536,128]{1,0:T(8,128)(2,1)} %get-tuple-element.43), channel_id=1, source_target_pairs={{0,2},{1,3},{2,0},{3,1},{4,6},{5,7},{6,4},{7,5},{8,10},{9,11},{10,... | collective-permute-start | bytes 1179656 | tf_op jit(solution)/shard_map/ppermute | solution.py:201
  28.9 1.6 %collective-permute-start.9 = (bf16[1536,128]{1,0:T(8,128)(2,1)}, bf16[1536,128]{1,0:T(8,128)(2,1)S(1)}, u32[]{:S(2)}, u32[]{:S(2)}) collective-permute-start(bf16[1536,128]{1,0:T(8,128)(2,1)} %get-tuple-element.41), channel_id=1, source_target_pairs={{0,3},{1,0},{2,1},{3,2},{4,7},{5,4},{6,5},{7,6},{8,11},{9,8},{10,9... | collective-permute-start | bytes 1179656 | tf_op jit(solution)/shard_map/ppermute | solution.py:201
  31.4 4.2 %densify.1.band = bf16[8,640,512]{2,1,0:T(8,128)(2,1)S(1)} custom-call(s32[160]{0:T(256)S(1)} %select_reduce_fusion.inv, bf16[1,1,544,128,128]{4,3,2,1,0:T(8,128)(2,1)} %tiles.1), custom_call_target="tpu_custom_call" | custom-call | flops 1024 | bytes 1024 | tf_op jit(solution)/shard_map/densify/pallas_call | solution.py:55
  35.6 2.3 %copy-done = bf16[8,640,512]{2,1,0:T(8,128)(2,1)} copy-done((bf16[8,640,512]{2,1,0:T(8,128)(2,1)}, bf16[8,640,512]{2,1,0:T(8,128)(2,1)S(1)}, u32[]{:S(2)}) %copy-start) | copy-done | bytes 5242904
  37.9 8.3 %collective-permute-done.8.g2.w2 = bf16[1536,128]{1,0:T(8,128)(2,1)S(1)} collective-permute-done((bf16[1536,128]{1,0:T(8,128)(2,1)}, bf16[1536,128]{1,0:T(8,128)(2,1)S(1)}, u32[]{:S(2)}, u32[]{:S(2)}) %collective-permute-start.8) | collective-permute-done | bytes 393248 | tf_op jit(solution)/shard_map/ppermute | solution.py:201
  46.3 1.8 %outer.1 = bf16[32,4,16,128]{3,2,1,0:T(8,128)(2,1)} custom-call(s32[1]{0:T(128)} %bitcast.depth, bf16[1536,128]{1,0:T(8,128)(2,1)S(1)} %get-tuple-element.44.g0.w0, bf16[1536,128]{1,0:T(8,128)(2,1)S(1)} %collective-permute-done.7.g1.w1, bf16[1536,128]{1,0:T(8,128)(2,1)S(1)} %collective-permute-done.8.g2.w2, ...), custom_call_target="tpu_custom_call" | custom-call | flops 1024 | bytes 1024 | tf_op jit(solution)/shard_map/outer/pallas_call | solution.py:153
  48.1 9.9 %all-to-all-start = ((bf16[128,16,128]{2,1,0:T(8,128)(2,1)}), bf16[128,16,128]{2,1,0:T(8,128)(2,1)}, u32[]{:S(2)}, u32[]{:S(2)}) async-start(bf16[128,16,128]{2,1,0:T(8,128)(2,1)} %bitcast.2), calls=%async_computation | async-start | bytes 1048576 | tf_op jit(solution)/shard_map/all_to_all | solution.py:219
  58.0 2.5 %copy-done.1 = bf16[8,640,512]{2,1,0:T(8,128)(2,1)S(1)} copy-done((bf16[8,640,512]{2,1,0:T(8,128)(2,1)S(1)}, bf16[8,640,512]{2,1,0:T(8,128)(2,1)}, u32[]{:S(2)}) %copy-start.1) | copy-done | bytes 5242904
  61.5 6.3 %columns.1 = (bf16[1536,128]{1,0:T(8,128)(2,1)S(1)}, bf16[1536,128]{1,0:T(8,128)(2,1)}, bf16[1536,128]{1,0:T(8,128)(2,1)}, bf16[1536,128]{1,0:T(8,128)(2,1)}) custom-call(s32[1]{0:T(128)} %bitcast.depth, bf16[8,640,512]{2,1,0:T(8,128)(2,1)S(1)} %copy-done.1, bf16[1024,128]{1,0:T(8,128)(2,1)S(1)} %fusion.own, ...), custom_call_target="tpu_custom_call" | custom-call | flops 1024 | bytes 1024 | tf_op jit(solution)/shard_map/columns/pallas_call | solution.py:94
  68.7 2.7 %collective-permute-start.12 = (bf16[1536,128]{1,0:T(8,128)(2,1)}, bf16[1536,128]{1,0:T(8,128)(2,1)S(1)}, u32[]{:S(2)}, u32[]{:S(2)}) collective-permute-start(bf16[1536,128]{1,0:T(8,128)(2,1)} %get-tuple-element.27), channel_id=1, source_target_pairs={{0,2},{1,3},{2,0},{3,1},{4,6},{5,7},{6,4},{7,5},{8,10},{9,11},{10,... | collective-permute-start | bytes 1179656 | tf_op jit(solution)/shard_map/ppermute | solution.py:201
  71.5 1.4 %collective-permute-start.13 = (bf16[1536,128]{1,0:T(8,128)(2,1)}, bf16[1536,128]{1,0:T(8,128)(2,1)S(1)}, u32[]{:S(2)}, u32[]{:S(2)}) collective-permute-start(bf16[1536,128]{1,0:T(8,128)(2,1)} %get-tuple-element.28), channel_id=1, source_target_pairs={{0,3},{1,0},{2,1},{3,2},{4,7},{5,4},{6,5},{7,6},{8,11},{9,8},{10,9... | collective-permute-start | bytes 1179656 | tf_op jit(solution)/shard_map/ppermute | solution.py:201
  74.8 7.6 %all-to-all-start.1 = ((f32[32,16,128]{2,1,0:T(8,128)}), f32[32,16,128]{2,1,0:T(8,128)S(1)}, u32[]{:S(2)}, u32[]{:S(2)}) async-start(f32[32,16,128]{2,1,0:T(8,128)} %broadcast_in_dim.30), calls=%async_computation.1 | async-start | bytes 524288 | tf_op jit(solution)/shard_map/all_to_all | solution.py:233
  82.4 6.8 %collective-permute-done.12.r2 = bf16[1536,128]{1,0:T(8,128)(2,1)S(1)} collective-permute-done((bf16[1536,128]{1,0:T(8,128)(2,1)}, bf16[1536,128]{1,0:T(8,128)(2,1)S(1)}, u32[]{:S(2)}, u32[]{:S(2)}) %collective-permute-start.12) | collective-permute-done | bytes 393248 | tf_op jit(solution)/shard_map/ppermute | solution.py:201
  89.3 4.0 %collective-permute-start.14 = (bf16[256,128]{1,0:T(8,128)(2,1)S(1)}, bf16[256,128]{1,0:T(8,128)(2,1)S(1)}, u32[]{:S(2)}, u32[]{:S(2)}) collective-permute-start(bf16[256,128]{1,0:T(8,128)(2,1)S(1)} %get-tuple-element.36), channel_id=1, source_target_pairs={{0,112},{16,0},{32,16},{48,32},{64,48},{80,64},{96,80},{112,96},{1... | collective-permute-start | bytes 196616 | tf_op jit(solution)/shard_map/ppermute | solution.py:229
  93.2 1.9 %collective-permute-done.14.following = bf16[256,128]{1,0:T(8,128)(2,1)S(1)} collective-permute-done((bf16[256,128]{1,0:T(8,128)(2,1)S(1)}, bf16[256,128]{1,0:T(8,128)(2,1)S(1)}, u32[]{:S(2)}, u32[]{:S(2)}) %collective-permute-start.14) | collective-permute-done | bytes 65568 | tf_op jit(solution)/shard_map/ppermute | solution.py:229
  95.2 4.5 %collective-permute-done.15.previous = bf16[256,128]{1,0:T(8,128)(2,1)S(1)} collective-permute-done((bf16[256,128]{1,0:T(8,128)(2,1)S(1)}, bf16[256,128]{1,0:T(8,128)(2,1)S(1)}, u32[]{:S(2)}, u32[]{:S(2)}) %collective-permute-start.15) | collective-permute-done | bytes 65568 | tf_op jit(solution)/shard_map/ppermute | solution.py:230
  99.6 1.2 %place.1 = (bf16[4,1024,128]{2,1,0:T(8,128)(2,1)}, f32[512,128]{1,0:T(8,128)}) custom-call(s32[1]{0:T(128)} %bitcast.depth, bf16[1536,128]{1,0:T(8,128)(2,1)S(1)} %get-tuple-element.25.r0, bf16[1536,128]{1,0:T(8,128)(2,1)S(1)} %collective-permute-done.11.r1, bf16[1536,128]{1,0:T(8,128)(2,1)S(1)} %collective-permute-done.12.r2, ...), custom_call_target="tpu_custom_call" | custom-call | flops 1024 | bytes 1024 | tf_op jit(solution)/shard_map/place/pallas_call | solution.py:124
  (47 shorter events, 9.0 us)
Async XLA Ops:
  1.8 11.7 %collective-permute-start.3 = (bf16[1024,128]{1,0:T(8,128)(2,1)S(1)}, bf16[1024,128]{1,0:T(8,128)(2,1)S(1)}, u32[]{:S(2)}, u32[]{:S(2)}) collective-permute-start(bf16[1024,128]{1,0:T(8,128)(2,1)S(1)} %fusion.own), channel_id=1, source_target_pairs={{0,8},{4,12},{8,0},{12,4},{1,9},{5,13},{9,1},{13,5},{2,10},{6,14},... | collective-permute-start | bytes 786440 | tf_op jit(solution)/shard_map/ppermute | solution.py:187
  7.7 16.5 %copy-start.4 = (bf16[4096,128]{1,0:T(8,128)(2,1)S(1)}, bf16[4096,128]{1,0:T(8,128)(2,1)}, u32[]{:S(2)}) copy-start(bf16[4096,128]{1,0:T(8,128)(2,1)} %param.10) | copy-start | bytes 3145732
  7.7 9.4 %collective-permute-start = (bf16[1024,128]{1,0:T(8,128)(2,1)S(1)}, bf16[1024,128]{1,0:T(8,128)(2,1)S(1)}, u32[]{:S(2)}, u32[]{:S(2)}) collective-permute-start(bf16[1024,128]{1,0:T(8,128)(2,1)S(1)} %get-tuple-element.34), channel_id=1, source_target_pairs={{0,1},{1,2},{2,3},{3,0},{4,5},{5,6},{6,7},{7,4},{8,9},{9,10},{10,1... | collective-permute-start | bytes 786440 | tf_op jit(solution)/shard_map/ppermute | solution.py:201
  9.3 14.3 %collective-permute-start.1 = (bf16[1024,128]{1,0:T(8,128)(2,1)S(1)}, bf16[1024,128]{1,0:T(8,128)(2,1)S(1)}, u32[]{:S(2)}, u32[]{:S(2)}) collective-permute-start(bf16[1024,128]{1,0:T(8,128)(2,1)S(1)} %get-tuple-element.33), channel_id=1, source_target_pairs={{0,2},{1,3},{2,0},{3,1},{4,6},{5,7},{6,4},{7,5},{8,10},{9,11},{10,... | collective-permute-start | bytes 786440 | tf_op jit(solution)/shard_map/ppermute | solution.py:201
  12.2 11.4 %collective-permute-start.2 = (bf16[1024,128]{1,0:T(8,128)(2,1)S(1)}, bf16[1024,128]{1,0:T(8,128)(2,1)S(1)}, u32[]{:S(2)}, u32[]{:S(2)}) collective-permute-start(bf16[1024,128]{1,0:T(8,128)(2,1)S(1)} %get-tuple-element.32), channel_id=1, source_target_pairs={{0,3},{1,0},{2,1},{3,2},{4,7},{5,4},{6,5},{7,6},{8,11},{9,8},{10,9... | collective-permute-start | bytes 786440 | tf_op jit(solution)/shard_map/ppermute | solution.py:201
  14.4 9.8 %copy-start.5 = (bf16[512,128]{1,0:T(8,128)(2,1)S(1)}, bf16[512,128]{1,0:T(8,128)(2,1)}, u32[]{:S(2)}) copy-start(bf16[512,128]{1,0:T(8,128)(2,1)} %param.11) | copy-start | bytes 393220
  17.1 20.9 %collective-permute-start.4 = (bf16[2048,128]{1,0:T(8,128)(2,1)}, bf16[2048,128]{1,0:T(8,128)(2,1)S(1)}, u32[]{:S(2)}, u32[]{:S(2)}) collective-permute-start(bf16[2048,128]{1,0:T(8,128)(2,1)} %pad_maximum_fusion.4), channel_id=1, source_target_pairs={{0,4},{4,0},{8,12},{12,8},{1,5},{5,1},{9,13},{13,9},{2,6},{6,2},{1... | collective-permute-start | bytes 1572872 | tf_op jit(solution)/shard_map/ppermute | solution.py:190
  23.7 6.8 %copy-start.6 = (s32[1,1,544]{2,1,0:T(1,128)S(1)}, s32[1,1,544]{2,1,0:T(1,128)}, u32[]{:S(2)}) copy-start(s32[1,1,544]{2,1,0:T(1,128)} %param.13) | copy-start | bytes 6532
  23.7 6.8 %copy-start.7 = (s32[1,1,544]{2,1,0:T(1,128)S(1)}, s32[1,1,544]{2,1,0:T(1,128)}, u32[]{:S(2)}) copy-start(s32[1,1,544]{2,1,0:T(1,128)} %param.14) | copy-start | bytes 6532
  23.7 24.4 %collective-permute-start.6 = (bf16[3072,128]{1,0:T(8,128)(2,1)S(1)}, bf16[3072,128]{1,0:T(8,128)(2,1)}, u32[]{:S(2)}, u32[]{:S(2)}) collective-permute-start(bf16[3072,128]{1,0:T(8,128)(2,1)S(1)} %constant_dynamic-update-slice_fusion.more.f0), channel_id=1, source_target_pairs={{0,8},{4,12},{8,0},{12,4},{1,9},{5,13},{9,1},{13,5},{2,10},{6,14},... | collective-permute-start | bytes 2359304 | tf_op jit(solution)/shard_map/ppermute | solution.py:187
  25.3 12.6 %collective-permute-start.7 = (bf16[1536,128]{1,0:T(8,128)(2,1)}, bf16[1536,128]{1,0:T(8,128)(2,1)S(1)}, u32[]{:S(2)}, u32[]{:S(2)}) collective-permute-start(bf16[1536,128]{1,0:T(8,128)(2,1)} %get-tuple-element.42), channel_id=1, source_target_pairs={{0,1},{1,2},{2,3},{3,0},{4,5},{5,6},{6,7},{7,4},{8,9},{9,10},{10,1... | collective-permute-start | bytes 1179656 | tf_op jit(solution)/shard_map/ppermute | solution.py:201
  26.5 19.8 %collective-permute-start.8 = (bf16[1536,128]{1,0:T(8,128)(2,1)}, bf16[1536,128]{1,0:T(8,128)(2,1)S(1)}, u32[]{:S(2)}, u32[]{:S(2)}) collective-permute-start(bf16[1536,128]{1,0:T(8,128)(2,1)} %get-tuple-element.43), channel_id=1, source_target_pairs={{0,2},{1,3},{2,0},{3,1},{4,6},{5,7},{6,4},{7,5},{8,10},{9,11},{10,... | collective-permute-start | bytes 1179656 | tf_op jit(solution)/shard_map/ppermute | solution.py:201
  28.9 17.4 %collective-permute-start.9 = (bf16[1536,128]{1,0:T(8,128)(2,1)}, bf16[1536,128]{1,0:T(8,128)(2,1)S(1)}, u32[]{:S(2)}, u32[]{:S(2)}) collective-permute-start(bf16[1536,128]{1,0:T(8,128)(2,1)} %get-tuple-element.41), channel_id=1, source_target_pairs={{0,3},{1,0},{2,1},{3,2},{4,7},{5,4},{6,5},{7,6},{8,11},{9,8},{10,9... | collective-permute-start | bytes 1179656 | tf_op jit(solution)/shard_map/ppermute | solution.py:201
  37.9 10.2 %copy-start.2 = (bf16[2048,128]{1,0:T(8,128)(2,1)}, bf16[2048,128]{1,0:T(8,128)(2,1)S(1)}, u32[]{:S(2)}) copy-start(bf16[2048,128]{1,0:T(8,128)(2,1)S(1)} %collective-permute-done.4.pair) | copy-start | bytes 1572868
  37.9 20.0 %collective-permute-start.5 = (bf16[3072,128]{1,0:T(8,128)(2,1)S(1)}, bf16[3072,128]{1,0:T(8,128)(2,1)}, u32[]{:S(2)}, u32[]{:S(2)}) collective-permute-start(bf16[3072,128]{1,0:T(8,128)(2,1)S(1)} %constant_dynamic-update-slice_fusion.more.f0), channel_id=1, source_target_pairs={{0,4},{4,0},{8,12},{12,8},{1,5},{5,1},{9,13},{13,9},{2,6},{6,2},{1... | collective-permute-start | bytes 2359304 | tf_op jit(solution)/shard_map/ppermute | solution.py:190
  48.1 9.9 %collective-permute-start.10 = (bf16[3072,128]{1,0:T(8,128)(2,1)}, bf16[3072,128]{1,0:T(8,128)(2,1)}, u32[]{:S(2)}, u32[]{:S(2)}) collective-permute-start(bf16[3072,128]{1,0:T(8,128)(2,1)} %collective-permute-done.6.f2), channel_id=1, source_target_pairs={{0,4},{4,0},{8,12},{12,8},{1,5},{5,1},{9,13},{13,9},{2,6},{6,2},{1... | collective-permute-start | bytes 2359304 | tf_op jit(solution)/shard_map/ppermute | solution.py:190
  48.1 24.8 %all-to-all-start = ((bf16[128,16,128]{2,1,0:T(8,128)(2,1)}), bf16[128,16,128]{2,1,0:T(8,128)(2,1)}, u32[]{:S(2)}, u32[]{:S(2)}) async-start(bf16[128,16,128]{2,1,0:T(8,128)(2,1)} %bitcast.2), calls=%async_computation | async-start | bytes 1048576 | tf_op jit(solution)/shard_map/all_to_all | solution.py:219
  58.0 2.5 %copy-start.1 = (bf16[8,640,512]{2,1,0:T(8,128)(2,1)S(1)}, bf16[8,640,512]{2,1,0:T(8,128)(2,1)}, u32[]{:S(2)}) copy-start(bf16[8,640,512]{2,1,0:T(8,128)(2,1)} %copy-done) | copy-start | bytes 15728644
  67.9 14.5 %collective-permute-start.11 = (bf16[1536,128]{1,0:T(8,128)(2,1)}, bf16[1536,128]{1,0:T(8,128)(2,1)S(1)}, u32[]{:S(2)}, u32[]{:S(2)}) collective-permute-start(bf16[1536,128]{1,0:T(8,128)(2,1)} %get-tuple-element.26), channel_id=1, source_target_pairs={{0,1},{1,2},{2,3},{3,0},{4,5},{5,6},{6,7},{7,4},{8,9},{9,10},{10,1... | collective-permute-start | bytes 1179656 | tf_op jit(solution)/shard_map/ppermute | solution.py:201
  68.7 20.5 %collective-permute-start.12 = (bf16[1536,128]{1,0:T(8,128)(2,1)}, bf16[1536,128]{1,0:T(8,128)(2,1)S(1)}, u32[]{:S(2)}, u32[]{:S(2)}) collective-permute-start(bf16[1536,128]{1,0:T(8,128)(2,1)} %get-tuple-element.27), channel_id=1, source_target_pairs={{0,2},{1,3},{2,0},{3,1},{4,6},{5,7},{6,4},{7,5},{8,10},{9,11},{10,... | collective-permute-start | bytes 1179656 | tf_op jit(solution)/shard_map/ppermute | solution.py:201
  71.5 17.8 %collective-permute-start.13 = (bf16[1536,128]{1,0:T(8,128)(2,1)}, bf16[1536,128]{1,0:T(8,128)(2,1)S(1)}, u32[]{:S(2)}, u32[]{:S(2)}) collective-permute-start(bf16[1536,128]{1,0:T(8,128)(2,1)} %get-tuple-element.28), channel_id=1, source_target_pairs={{0,3},{1,0},{2,1},{3,2},{4,7},{5,4},{6,5},{7,6},{8,11},{9,8},{10,9... | collective-permute-start | bytes 1179656 | tf_op jit(solution)/shard_map/ppermute | solution.py:201
  74.8 18.5 %all-to-all-start.1 = ((f32[32,16,128]{2,1,0:T(8,128)}), f32[32,16,128]{2,1,0:T(8,128)S(1)}, u32[]{:S(2)}, u32[]{:S(2)}) async-start(f32[32,16,128]{2,1,0:T(8,128)} %broadcast_in_dim.30), calls=%async_computation.1 | async-start | bytes 524288 | tf_op jit(solution)/shard_map/all_to_all | solution.py:233
  89.3 5.9 %collective-permute-start.14 = (bf16[256,128]{1,0:T(8,128)(2,1)S(1)}, bf16[256,128]{1,0:T(8,128)(2,1)S(1)}, u32[]{:S(2)}, u32[]{:S(2)}) collective-permute-start(bf16[256,128]{1,0:T(8,128)(2,1)S(1)} %get-tuple-element.36), channel_id=1, source_target_pairs={{0,112},{16,0},{32,16},{48,32},{64,48},{80,64},{96,80},{112,96},{1... | collective-permute-start | bytes 196616 | tf_op jit(solution)/shard_map/ppermute | solution.py:229
  93.2 6.4 %collective-permute-start.15 = (bf16[256,128]{1,0:T(8,128)(2,1)S(1)}, bf16[256,128]{1,0:T(8,128)(2,1)S(1)}, u32[]{:S(2)}, u32[]{:S(2)}) collective-permute-start(bf16[256,128]{1,0:T(8,128)(2,1)S(1)} %get-tuple-element.35), channel_id=1, source_target_pairs={{0,16},{16,32},{32,48},{48,64},{64,80},{80,96},{96,112},{112,0},{1... | collective-permute-start | bytes 196616 | tf_op jit(solution)/shard_map/ppermute | solution.py:230
  (2 other events, 3.4 us)

commit v5 on v4

--- a/solution.py
+++ b/solution.py
@@ -70,6 +70,15 @@
         src = pl.ds(pl.multiple_of(8 * T + (depth[0] + t) % 4 * T, T), T)
         for s, w in enumerate((w0, w1, w2, w3)):
             weight[t * T:(t + 1) * T, s * T:(s + 1) * T] = w[src, :]
+
+    def finish(k):
+        rows = slice(k * 2 * T, (k + 1) * 2 * T)
+        got = lax.dot_general(
+            acc[rows, :].astype(bf16), weight[...], (((1,), (1,)), ((), ())), preferred_element_type=f32
+        ).astype(bf16)
+        for t in range(4):
+            parts[t][rows, :] = got[:, t * T:(t + 1) * T]
+
     for q in range(QUADS):
         here, later = slice(q * T, (q + 1) * T), slice((8 + q) * T, (9 + q) * T)
         sides = [jnp.concatenate([own[here], pair[here], zed[here], pair[later]], axis=0)]
@@ -81,13 +90,10 @@
         if seen:
             acc[q * T:(q + seen) * T, :] += got[0:seen * T]
         acc[(q + seen) * T:(q + SLOTS) * T, :] = got[seen * T:SLOTS * T]
-    for k in range(6):
-        rows = slice(k * 2 * T, (k + 1) * 2 * T)
-        got = lax.dot_general(
-            acc[rows, :].astype(bf16), weight[...], (((1,), (1,)), ((), ())), preferred_element_type=f32
-        ).astype(bf16)
-        for t in range(4):
-            parts[t][rows, :] = got[:, t * T:(t + 1) * T]
+        if q % 2:
+            finish(q // 2)
+    finish(4)
+    finish(5)
 
 
 def columns(depth, band, near, far, given):

time: 101 us -> 101 us (level)
  no operation moved by 1% of the time
where the time goes in v5:
time: 101 us
  starting transfers between devices  42 us (42%)
  waiting for transfers between devices  30.7 us (30%)
  Pallas kernels  13.6 us (13%)
  local copies, waits for them, and re-layouts  6.75 us (7%)
  other arithmetic  6.33 us (6%)
  between operations  1.49 us (1%)
    ppermute x9, waiting for transfers between devices, from_depth(): return lax.ppermute(array, 'depth', ring(4, t))  24.3 us
    ppermute x9, starting transfers between devices, from_depth(): return lax.ppermute(array, 'depth', ring(4, t))  16.1 us
    all_to_all x1, starting transfers between devices, local(): pieces = lax.all_to_all(pieces, ('row', 'col', 'depth'), 0, 0)  9.88 us
    all_to_all x1, starting transfers between devices, local(): lax.all_to_all(jnp.broadcast_to(piece, (32, 16, T)), RC, 0, 0)  7.59 us
    pallas_call x1, Pallas kernels, columns(): pl.pallas_call(columns_kernel, in_specs=[SMEM] + [VMEM] * 12, out_specs=[...  6.32 us
    unnamed x18, local copies, waits for them, and re-layouts  5.92 us
    ppermute x1, waiting for transfers between devices, local(): lax.ppermute(of_quarter(3, slice(10 * T, 12 * T)), 'row', ring(8, 1))  4.47 us
    ppermute x2, starting transfers between devices, other(): return lax.ppermute(array, 'col', flip(2))  4.47 us
  transfers between devices with their start and end apart: 18, of which 6 were waited for; matrix products, arithmetic and copies ran while one was open for 6% of the time, Pallas kernels for 12%

profile of v5, /device:TPU:0, one launch (start us, length us, event | category | flops | bytes accessed | tf_op | source)
XLA Modules:
  0.0 100.8 jit_solution(17416099514072380911)
XLA Ops:
  1.8 4.0 %collective-permute-start.3 = (bf16[1024,128]{1,0:T(8,128)(2,1)S(1)}, bf16[1024,128]{1,0:T(8,128)(2,1)S(1)}, u32[]{:S(2)}, u32[]{:S(2)}) collective-permute-start(bf16[1024,128]{1,0:T(8,128)(2,1)S(1)} %fusion.own), channel_id=1, source_target_pairs={{0,8},{4,12},{8,0},{12,4},{1,9},{5,13},{9,1},{13,5},{2,10},{6,14},... | collective-permute-start | bytes 786440 | tf_op jit(solution)/shard_map/ppermute | solution.py:193
  5.9 1.8 %fusion.3 = (bf16[1024,128]{1,0:T(8,128)(2,1)S(1)}, bf16[1024,128]{1,0:T(8,128)(2,1)S(1)}, bf16[1024,128]{1,0:T(8,128)(2,1)S(1)}) fusion(s32[4096,128]{1,0:T(8,128)} %param.9, s32[]{:T(128)S(6)} %select_n.191, bf16[4096,128]{1,0:T(8,128)(2,1)} %param.8, s32[]{:T(128)S(6)} %select_n.188, s32[]{:T(128)S(6)} %select_n.185), kind=kLoop, calls=%fused_computation.13 | loop fusion | flops 786432 | bytes 3145740 | tf_op jit(solution)/shard_map/jit(_where)/select_n | solution.py:204
  7.7 1.6 %collective-permute-start = (bf16[1024,128]{1,0:T(8,128)(2,1)S(1)}, bf16[1024,128]{1,0:T(8,128)(2,1)S(1)}, u32[]{:S(2)}, u32[]{:S(2)}) collective-permute-start(bf16[1024,128]{1,0:T(8,128)(2,1)S(1)} %get-tuple-element.34), channel_id=1, source_target_pairs={{0,1},{1,2},{2,3},{3,0},{4,5},{5,6},{6,7},{7,4},{8,9},{9,10},{10,1... | collective-permute-start | bytes 786440 | tf_op jit(solution)/shard_map/ppermute | solution.py:207
  9.3 2.9 %collective-permute-start.1 = (bf16[1024,128]{1,0:T(8,128)(2,1)S(1)}, bf16[1024,128]{1,0:T(8,128)(2,1)S(1)}, u32[]{:S(2)}, u32[]{:S(2)}) collective-permute-start(bf16[1024,128]{1,0:T(8,128)(2,1)S(1)} %get-tuple-element.33), channel_id=1, source_target_pairs={{0,2},{1,3},{2,0},{3,1},{4,6},{5,7},{6,4},{7,5},{8,10},{9,11},{10,... | collective-permute-start | bytes 786440 | tf_op jit(solution)/shard_map/ppermute | solution.py:207
  12.2 1.3 %collective-permute-start.2 = (bf16[1024,128]{1,0:T(8,128)(2,1)S(1)}, bf16[1024,128]{1,0:T(8,128)(2,1)S(1)}, u32[]{:S(2)}, u32[]{:S(2)}) collective-permute-start(bf16[1024,128]{1,0:T(8,128)(2,1)S(1)} %get-tuple-element.32), channel_id=1, source_target_pairs={{0,3},{1,0},{2,1},{3,2},{4,7},{5,4},{6,5},{7,6},{8,11},{9,8},{10,9... | collective-permute-start | bytes 786440 | tf_op jit(solution)/shard_map/ppermute | solution.py:207
  14.4 2.7 %collective-permute-done = bf16[1024,128]{1,0:T(8,128)(2,1)S(1)} collective-permute-done((bf16[1024,128]{1,0:T(8,128)(2,1)S(1)}, bf16[1024,128]{1,0:T(8,128)(2,1)S(1)}, u32[]{:S(2)}, u32[]{:S(2)}) %collective-permute-start) | collective-permute-done | bytes 262176 | tf_op jit(solution)/shard_map/ppermute | solution.py:207
  17.1 6.5 %collective-permute-done.1 = bf16[1024,128]{1,0:T(8,128)(2,1)S(1)} collective-permute-done((bf16[1024,128]{1,0:T(8,128)(2,1)S(1)}, bf16[1024,128]{1,0:T(8,128)(2,1)S(1)}, u32[]{:S(2)}, u32[]{:S(2)}) %collective-permute-start.1) | collective-permute-done | bytes 262176 | tf_op jit(solution)/shard_map/ppermute | solution.py:207
  26.5 2.4 %collective-permute-start.8 = (bf16[1536,128]{1,0:T(8,128)(2,1)}, bf16[1536,128]{1,0:T(8,128)(2,1)S(1)}, u32[]{:S(2)}, u32[]{:S(2)}) collective-permute-start(bf16[1536,128]{1,0:T(8,128)(2,1)} %get-tuple-element.43), channel_id=1, source_target_pairs={{0,2},{1,3},{2,0},{3,1},{4,6},{5,7},{6,4},{7,5},{8,10},{9,11},{10,... | collective-permute-start | bytes 1179656 | tf_op jit(solution)/shard_map/ppermute | solution.py:207
  28.9 1.6 %collective-permute-start.9 = (bf16[1536,128]{1,0:T(8,128)(2,1)}, bf16[1536,128]{1,0:T(8,128)(2,1)S(1)}, u32[]{:S(2)}, u32[]{:S(2)}) collective-permute-start(bf16[1536,128]{1,0:T(8,128)(2,1)} %get-tuple-element.41), channel_id=1, source_target_pairs={{0,3},{1,0},{2,1},{3,2},{4,7},{5,4},{6,5},{7,6},{8,11},{9,8},{10,9... | collective-permute-start | bytes 1179656 | tf_op jit(solution)/shard_map/ppermute | solution.py:207
  31.4 4.3 %densify.1.band = bf16[8,640,512]{2,1,0:T(8,128)(2,1)S(1)} custom-call(s32[160]{0:T(256)S(1)} %select_reduce_fusion.inv, bf16[1,1,544,128,128]{4,3,2,1,0:T(8,128)(2,1)} %tiles.1), custom_call_target="tpu_custom_call" | custom-call | flops 1024 | bytes 1024 | tf_op jit(solution)/shard_map/densify/pallas_call | solution.py:55
  35.7 2.3 %copy-done = bf16[8,640,512]{2,1,0:T(8,128)(2,1)} copy-done((bf16[8,640,512]{2,1,0:T(8,128)(2,1)}, bf16[8,640,512]{2,1,0:T(8,128)(2,1)S(1)}, u32[]{:S(2)}) %copy-start) | copy-done | bytes 5242904
  38.0 8.3 %collective-permute-done.8.g2.w2 = bf16[1536,128]{1,0:T(8,128)(2,1)S(1)} collective-permute-done((bf16[1536,128]{1,0:T(8,128)(2,1)}, bf16[1536,128]{1,0:T(8,128)(2,1)S(1)}, u32[]{:S(2)}, u32[]{:S(2)}) %collective-permute-start.8) | collective-permute-done | bytes 393248 | tf_op jit(solution)/shard_map/ppermute | solution.py:207
  46.3 1.8 %outer.1 = bf16[32,4,16,128]{3,2,1,0:T(8,128)(2,1)} custom-call(s32[1]{0:T(128)} %bitcast.depth, bf16[1536,128]{1,0:T(8,128)(2,1)S(1)} %get-tuple-element.44.g0.w0, bf16[1536,128]{1,0:T(8,128)(2,1)S(1)} %collective-permute-done.7.g1.w1, bf16[1536,128]{1,0:T(8,128)(2,1)S(1)} %collective-permute-done.8.g2.w2, ...), custom_call_target="tpu_custom_call" | custom-call | flops 1024 | bytes 1024 | tf_op jit(solution)/shard_map/outer/pallas_call | solution.py:159
  48.1 9.9 %all-to-all-start = ((bf16[128,16,128]{2,1,0:T(8,128)(2,1)}), bf16[128,16,128]{2,1,0:T(8,128)(2,1)}, u32[]{:S(2)}, u32[]{:S(2)}) async-start(bf16[128,16,128]{2,1,0:T(8,128)(2,1)} %bitcast.2), calls=%async_computation | async-start | bytes 1048576 | tf_op jit(solution)/shard_map/all_to_all | solution.py:225
  58.0 2.5 %copy-done.1 = bf16[8,640,512]{2,1,0:T(8,128)(2,1)S(1)} copy-done((bf16[8,640,512]{2,1,0:T(8,128)(2,1)S(1)}, bf16[8,640,512]{2,1,0:T(8,128)(2,1)}, u32[]{:S(2)}) %copy-start.1) | copy-done | bytes 5242904
  61.5 6.3 %columns.1 = (bf16[1536,128]{1,0:T(8,128)(2,1)S(1)}, bf16[1536,128]{1,0:T(8,128)(2,1)}, bf16[1536,128]{1,0:T(8,128)(2,1)}, bf16[1536,128]{1,0:T(8,128)(2,1)}) custom-call(s32[1]{0:T(128)} %bitcast.depth, bf16[8,640,512]{2,1,0:T(8,128)(2,1)S(1)} %copy-done.1, bf16[1024,128]{1,0:T(8,128)(2,1)S(1)} %fusion.own, ...), custom_call_target="tpu_custom_call" | custom-call | flops 1024 | bytes 1024 | tf_op jit(solution)/shard_map/columns/pallas_call | solution.py:100
  68.7 2.7 %collective-permute-start.12 = (bf16[1536,128]{1,0:T(8,128)(2,1)}, bf16[1536,128]{1,0:T(8,128)(2,1)S(1)}, u32[]{:S(2)}, u32[]{:S(2)}) collective-permute-start(bf16[1536,128]{1,0:T(8,128)(2,1)} %get-tuple-element.27), channel_id=1, source_target_pairs={{0,2},{1,3},{2,0},{3,1},{4,6},{5,7},{6,4},{7,5},{8,10},{9,11},{10,... | collective-permute-start | bytes 1179656 | tf_op jit(solution)/shard_map/ppermute | solution.py:207
  71.5 1.4 %collective-permute-start.13 = (bf16[1536,128]{1,0:T(8,128)(2,1)}, bf16[1536,128]{1,0:T(8,128)(2,1)S(1)}, u32[]{:S(2)}, u32[]{:S(2)}) collective-permute-start(bf16[1536,128]{1,0:T(8,128)(2,1)} %get-tuple-element.28), channel_id=1, source_target_pairs={{0,3},{1,0},{2,1},{3,2},{4,7},{5,4},{6,5},{7,6},{8,11},{9,8},{10,9... | collective-permute-start | bytes 1179656 | tf_op jit(solution)/shard_map/ppermute | solution.py:207
  74.8 7.6 %all-to-all-start.1 = ((f32[32,16,128]{2,1,0:T(8,128)}), f32[32,16,128]{2,1,0:T(8,128)S(1)}, u32[]{:S(2)}, u32[]{:S(2)}) async-start(f32[32,16,128]{2,1,0:T(8,128)} %broadcast_in_dim.30), calls=%async_computation.1 | async-start | bytes 524288 | tf_op jit(solution)/shard_map/all_to_all | solution.py:239
  82.4 6.8 %collective-permute-done.12.r2 = bf16[1536,128]{1,0:T(8,128)(2,1)S(1)} collective-permute-done((bf16[1536,128]{1,0:T(8,128)(2,1)}, bf16[1536,128]{1,0:T(8,128)(2,1)S(1)}, u32[]{:S(2)}, u32[]{:S(2)}) %collective-permute-start.12) | collective-permute-done | bytes 393248 | tf_op jit(solution)/shard_map/ppermute | solution.py:207
  89.3 4.0 %collective-permute-start.14 = (bf16[256,128]{1,0:T(8,128)(2,1)S(1)}, bf16[256,128]{1,0:T(8,128)(2,1)S(1)}, u32[]{:S(2)}, u32[]{:S(2)}) collective-permute-start(bf16[256,128]{1,0:T(8,128)(2,1)S(1)} %get-tuple-element.36), channel_id=1, source_target_pairs={{0,112},{16,0},{32,16},{48,32},{64,48},{80,64},{96,80},{112,96},{1... | collective-permute-start | bytes 196616 | tf_op jit(solution)/shard_map/ppermute | solution.py:235
  93.2 1.9 %collective-permute-done.14.following = bf16[256,128]{1,0:T(8,128)(2,1)S(1)} collective-permute-done((bf16[256,128]{1,0:T(8,128)(2,1)S(1)}, bf16[256,128]{1,0:T(8,128)(2,1)S(1)}, u32[]{:S(2)}, u32[]{:S(2)}) %collective-permute-start.14) | collective-permute-done | bytes 65568 | tf_op jit(solution)/shard_map/ppermute | solution.py:235
  95.1 4.5 %collective-permute-done.15.previous = bf16[256,128]{1,0:T(8,128)(2,1)S(1)} collective-permute-done((bf16[256,128]{1,0:T(8,128)(2,1)S(1)}, bf16[256,128]{1,0:T(8,128)(2,1)S(1)}, u32[]{:S(2)}, u32[]{:S(2)}) %collective-permute-start.15) | collective-permute-done | bytes 65568 | tf_op jit(solution)/shard_map/ppermute | solution.py:236
  99.6 1.2 %place.1 = (bf16[4,1024,128]{2,1,0:T(8,128)(2,1)}, f32[512,128]{1,0:T(8,128)}) custom-call(s32[1]{0:T(128)} %bitcast.depth, bf16[1536,128]{1,0:T(8,128)(2,1)S(1)} %get-tuple-element.25.r0, bf16[1536,128]{1,0:T(8,128)(2,1)S(1)} %collective-permute-done.11.r1, bf16[1536,128]{1,0:T(8,128)(2,1)S(1)} %collective-permute-done.12.r2, ...), custom_call_target="tpu_custom_call" | custom-call | flops 1024 | bytes 1024 | tf_op jit(solution)/shard_map/place/pallas_call | solution.py:130
  (47 shorter events, 9.0 us)
Async XLA Ops:
  1.8 11.7 %collective-permute-start.3 = (bf16[1024,128]{1,0:T(8,128)(2,1)S(1)}, bf16[1024,128]{1,0:T(8,128)(2,1)S(1)}, u32[]{:S(2)}, u32[]{:S(2)}) collective-permute-start(bf16[1024,128]{1,0:T(8,128)(2,1)S(1)} %fusion.own), channel_id=1, source_target_pairs={{0,8},{4,12},{8,0},{12,4},{1,9},{5,13},{9,1},{13,5},{2,10},{6,14},... | collective-permute-start | bytes 786440 | tf_op jit(solution)/shard_map/ppermute | solution.py:193
  7.7 16.5 %copy-start.4 = (bf16[4096,128]{1,0:T(8,128)(2,1)S(1)}, bf16[4096,128]{1,0:T(8,128)(2,1)}, u32[]{:S(2)}) copy-start(bf16[4096,128]{1,0:T(8,128)(2,1)} %param.10) | copy-start | bytes 3145732
  7.7 9.4 %collective-permute-start = (bf16[1024,128]{1,0:T(8,128)(2,1)S(1)}, bf16[1024,128]{1,0:T(8,128)(2,1)S(1)}, u32[]{:S(2)}, u32[]{:S(2)}) collective-permute-start(bf16[1024,128]{1,0:T(8,128)(2,1)S(1)} %get-tuple-element.34), channel_id=1, source_target_pairs={{0,1},{1,2},{2,3},{3,0},{4,5},{5,6},{6,7},{7,4},{8,9},{9,10},{10,1... | collective-permute-start | bytes 786440 | tf_op jit(solution)/shard_map/ppermute | solution.py:207
  9.3 14.3 %collective-permute-start.1 = (bf16[1024,128]{1,0:T(8,128)(2,1)S(1)}, bf16[1024,128]{1,0:T(8,128)(2,1)S(1)}, u32[]{:S(2)}, u32[]{:S(2)}) collective-permute-start(bf16[1024,128]{1,0:T(8,128)(2,1)S(1)} %get-tuple-element.33), channel_id=1, source_target_pairs={{0,2},{1,3},{2,0},{3,1},{4,6},{5,7},{6,4},{7,5},{8,10},{9,11},{10,... | collective-permute-start | bytes 786440 | tf_op jit(solution)/shard_map/ppermute | solution.py:207
  12.2 11.4 %collective-permute-start.2 = (bf16[1024,128]{1,0:T(8,128)(2,1)S(1)}, bf16[1024,128]{1,0:T(8,128)(2,1)S(1)}, u32[]{:S(2)}, u32[]{:S(2)}) collective-permute-start(bf16[1024,128]{1,0:T(8,128)(2,1)S(1)} %get-tuple-element.32), channel_id=1, source_target_pairs={{0,3},{1,0},{2,1},{3,2},{4,7},{5,4},{6,5},{7,6},{8,11},{9,8},{10,9... | collective-permute-start | bytes 786440 | tf_op jit(solution)/shard_map/ppermute | solution.py:207
  14.4 9.8 %copy-start.5 = (bf16[512,128]{1,0:T(8,128)(2,1)S(1)}, bf16[512,128]{1,0:T(8,128)(2,1)}, u32[]{:S(2)}) copy-start(bf16[512,128]{1,0:T(8,128)(2,1)} %param.11) | copy-start | bytes 393220
  17.1 20.9 %collective-permute-start.4 = (bf16[2048,128]{1,0:T(8,128)(2,1)}, bf16[2048,128]{1,0:T(8,128)(2,1)S(1)}, u32[]{:S(2)}, u32[]{:S(2)}) collective-permute-start(bf16[2048,128]{1,0:T(8,128)(2,1)} %pad_maximum_fusion.4), channel_id=1, source_target_pairs={{0,4},{4,0},{8,12},{12,8},{1,5},{5,1},{9,13},{13,9},{2,6},{6,2},{1... | collective-permute-start | bytes 1572872 | tf_op jit(solution)/shard_map/ppermute | solution.py:196
  23.7 6.8 %copy-start.6 = (s32[1,1,544]{2,1,0:T(1,128)S(1)}, s32[1,1,544]{2,1,0:T(1,128)}, u32[]{:S(2)}) copy-start(s32[1,1,544]{2,1,0:T(1,128)} %param.13) | copy-start | bytes 6532
  23.7 6.8 %copy-start.7 = (s32[1,1,544]{2,1,0:T(1,128)S(1)}, s32[1,1,544]{2,1,0:T(1,128)}, u32[]{:S(2)}) copy-start(s32[1,1,544]{2,1,0:T(1,128)} %param.14) | copy-start | bytes 6532
  23.7 24.4 %collective-permute-start.6 = (bf16[3072,128]{1,0:T(8,128)(2,1)S(1)}, bf16[3072,128]{1,0:T(8,128)(2,1)}, u32[]{:S(2)}, u32[]{:S(2)}) collective-permute-start(bf16[3072,128]{1,0:T(8,128)(2,1)S(1)} %constant_dynamic-update-slice_fusion.more.f0), channel_id=1, source_target_pairs={{0,8},{4,12},{8,0},{12,4},{1,9},{5,13},{9,1},{13,5},{2,10},{6,14},... | collective-permute-start | bytes 2359304 | tf_op jit(solution)/shard_map/ppermute | solution.py:193
  25.3 12.7 %collective-permute-start.7 = (bf16[1536,128]{1,0:T(8,128)(2,1)}, bf16[1536,128]{1,0:T(8,128)(2,1)S(1)}, u32[]{:S(2)}, u32[]{:S(2)}) collective-permute-start(bf16[1536,128]{1,0:T(8,128)(2,1)} %get-tuple-element.42), channel_id=1, source_target_pairs={{0,1},{1,2},{2,3},{3,0},{4,5},{5,6},{6,7},{7,4},{8,9},{9,10},{10,1... | collective-permute-start | bytes 1179656 | tf_op jit(solution)/shard_map/ppermute | solution.py:207
  26.5 19.8 %collective-permute-start.8 = (bf16[1536,128]{1,0:T(8,128)(2,1)}, bf16[1536,128]{1,0:T(8,128)(2,1)S(1)}, u32[]{:S(2)}, u32[]{:S(2)}) collective-permute-start(bf16[1536,128]{1,0:T(8,128)(2,1)} %get-tuple-element.43), channel_id=1, source_target_pairs={{0,2},{1,3},{2,0},{3,1},{4,6},{5,7},{6,4},{7,5},{8,10},{9,11},{10,... | collective-permute-start | bytes 1179656 | tf_op jit(solution)/shard_map/ppermute | solution.py:207
  28.9 17.4 %collective-permute-start.9 = (bf16[1536,128]{1,0:T(8,128)(2,1)}, bf16[1536,128]{1,0:T(8,128)(2,1)S(1)}, u32[]{:S(2)}, u32[]{:S(2)}) collective-permute-start(bf16[1536,128]{1,0:T(8,128)(2,1)} %get-tuple-element.41), channel_id=1, source_target_pairs={{0,3},{1,0},{2,1},{3,2},{4,7},{5,4},{6,5},{7,6},{8,11},{9,8},{10,9... | collective-permute-start | bytes 1179656 | tf_op jit(solution)/shard_map/ppermute | solution.py:207
  38.0 10.1 %copy-start.2 = (bf16[2048,128]{1,0:T(8,128)(2,1)}, bf16[2048,128]{1,0:T(8,128)(2,1)S(1)}, u32[]{:S(2)}) copy-start(bf16[2048,128]{1,0:T(8,128)(2,1)S(1)} %collective-permute-done.4.pair) | copy-start | bytes 1572868
  38.0 20.0 %collective-permute-start.5 = (bf16[3072,128]{1,0:T(8,128)(2,1)S(1)}, bf16[3072,128]{1,0:T(8,128)(2,1)}, u32[]{:S(2)}, u32[]{:S(2)}) collective-permute-start(bf16[3072,128]{1,0:T(8,128)(2,1)S(1)} %constant_dynamic-update-slice_fusion.more.f0), channel_id=1, source_target_pairs={{0,4},{4,0},{8,12},{12,8},{1,5},{5,1},{9,13},{13,9},{2,6},{6,2},{1... | collective-permute-start | bytes 2359304 | tf_op jit(solution)/shard_map/ppermute | solution.py:196
  48.1 9.9 %collective-permute-start.10 = (bf16[3072,128]{1,0:T(8,128)(2,1)}, bf16[3072,128]{1,0:T(8,128)(2,1)}, u32[]{:S(2)}, u32[]{:S(2)}) collective-permute-start(bf16[3072,128]{1,0:T(8,128)(2,1)} %collective-permute-done.6.f2), channel_id=1, source_target_pairs={{0,4},{4,0},{8,12},{12,8},{1,5},{5,1},{9,13},{13,9},{2,6},{6,2},{1... | collective-permute-start | bytes 2359304 | tf_op jit(solution)/shard_map/ppermute | solution.py:196
  48.1 24.8 %all-to-all-start = ((bf16[128,16,128]{2,1,0:T(8,128)(2,1)}), bf16[128,16,128]{2,1,0:T(8,128)(2,1)}, u32[]{:S(2)}, u32[]{:S(2)}) async-start(bf16[128,16,128]{2,1,0:T(8,128)(2,1)} %bitcast.2), calls=%async_computation | async-start | bytes 1048576 | tf_op jit(solution)/shard_map/all_to_all | solution.py:225
  58.0 2.5 %copy-start.1 = (bf16[8,640,512]{2,1,0:T(8,128)(2,1)S(1)}, bf16[8,640,512]{2,1,0:T(8,128)(2,1)}, u32[]{:S(2)}) copy-start(bf16[8,640,512]{2,1,0:T(8,128)(2,1)} %copy-done) | copy-start | bytes 15728644
  67.9 14.5 %collective-permute-start.11 = (bf16[1536,128]{1,0:T(8,128)(2,1)}, bf16[1536,128]{1,0:T(8,128)(2,1)S(1)}, u32[]{:S(2)}, u32[]{:S(2)}) collective-permute-start(bf16[1536,128]{1,0:T(8,128)(2,1)} %get-tuple-element.26), channel_id=1, source_target_pairs={{0,1},{1,2},{2,3},{3,0},{4,5},{5,6},{6,7},{7,4},{8,9},{9,10},{10,1... | collective-permute-start | bytes 1179656 | tf_op jit(solution)/shard_map/ppermute | solution.py:207
  68.7 20.5 %collective-permute-start.12 = (bf16[1536,128]{1,0:T(8,128)(2,1)}, bf16[1536,128]{1,0:T(8,128)(2,1)S(1)}, u32[]{:S(2)}, u32[]{:S(2)}) collective-permute-start(bf16[1536,128]{1,0:T(8,128)(2,1)} %get-tuple-element.27), channel_id=1, source_target_pairs={{0,2},{1,3},{2,0},{3,1},{4,6},{5,7},{6,4},{7,5},{8,10},{9,11},{10,... | collective-permute-start | bytes 1179656 | tf_op jit(solution)/shard_map/ppermute | solution.py:207
  71.5 17.8 %collective-permute-start.13 = (bf16[1536,128]{1,0:T(8,128)(2,1)}, bf16[1536,128]{1,0:T(8,128)(2,1)S(1)}, u32[]{:S(2)}, u32[]{:S(2)}) collective-permute-start(bf16[1536,128]{1,0:T(8,128)(2,1)} %get-tuple-element.28), channel_id=1, source_target_pairs={{0,3},{1,0},{2,1},{3,2},{4,7},{5,4},{6,5},{7,6},{8,11},{9,8},{10,9... | collective-permute-start | bytes 1179656 | tf_op jit(solution)/shard_map/ppermute | solution.py:207
  74.8 18.5 %all-to-all-start.1 = ((f32[32,16,128]{2,1,0:T(8,128)}), f32[32,16,128]{2,1,0:T(8,128)S(1)}, u32[]{:S(2)}, u32[]{:S(2)}) async-start(f32[32,16,128]{2,1,0:T(8,128)} %broadcast_in_dim.30), calls=%async_computation.1 | async-start | bytes 524288 | tf_op jit(solution)/shard_map/all_to_all | solution.py:239
  89.3 5.9 %collective-permute-start.14 = (bf16[256,128]{1,0:T(8,128)(2,1)S(1)}, bf16[256,128]{1,0:T(8,128)(2,1)S(1)}, u32[]{:S(2)}, u32[]{:S(2)}) collective-permute-start(bf16[256,128]{1,0:T(8,128)(2,1)S(1)} %get-tuple-element.36), channel_id=1, source_target_pairs={{0,112},{16,0},{32,16},{48,32},{64,48},{80,64},{96,80},{112,96},{1... | collective-permute-start | bytes 196616 | tf_op jit(solution)/shard_map/ppermute | solution.py:235
  93.2 6.4 %collective-permute-start.15 = (bf16[256,128]{1,0:T(8,128)(2,1)S(1)}, bf16[256,128]{1,0:T(8,128)(2,1)S(1)}, u32[]{:S(2)}, u32[]{:S(2)}) collective-permute-start(bf16[256,128]{1,0:T(8,128)(2,1)S(1)} %get-tuple-element.35), channel_id=1, source_target_pairs={{0,16},{16,32},{32,48},{48,64},{64,80},{80,96},{96,112},{112,0},{1... | collective-permute-start | bytes 196616 | tf_op jit(solution)/shard_map/ppermute | solution.py:236
  (2 other events, 3.4 us)
